TPU v7x, 32 devices: a whole 2x2x4 slice. The times are simulated.
32 devices in a mesh: row: 4 (over z), col: 8 (over y, x, core).
Axes of the slice: x: 2, y: 2, z: 4, core: 2. Of those that a mesh axis runs over, the one named last changes fastest.
Arguments:
- tokens: bfloat16 [512, 12288], P('col', 'row'), may hold values from -6 to 6
- up_weight: bfloat16 [12288, 24576], P('row', 'col'), may hold values from -0.109375 to 0.109375
- up_mask: int32 [192, 384], P('row', 'col'), may hold values 0 or 1
- down_weight: bfloat16 [24576, 12288], P('col', 'row'), may hold values from -0.078125 to 0.078125
- down_mask: int32 [384, 192], P('col', 'row'), may hold values 0 or 1
- grad_out: bfloat16 [512, 12288], P('col', 'row'), may hold values from -6 to 6
Outputs:
- out_heads: bfloat16 [96, 512, 128], P('row', 'col')
- grad_tokens: bfloat16 [512, 12288], P('col', 'row')
- grad_up: bfloat16 [12288, 24576], P('row', 'col')
- grad_down: bfloat16 [24576, 12288], P('col', 'row')
All inputs are finite; a program needn't handle non-finite values. No bound on the sum of `up_mask` or of `down_mask` on one device may be relied on, other than what follows from the above.
Results may differ from a plain program's by a relative error of at most 0.022.
Values may be sent and summed in bfloat16 or wider, within the bound.
No kernel may reach another device: no remote copies, remote signals or barrier semaphores. Data moves between devices by JAX's collectives and lax.ppermute only.
A program may use at most 320 MiB of HBM per device.

v0:
```python
import math

import jax
import jax.numpy as jnp
from jax import lax
from jax.sharding import PartitionSpec as P

BLOCK = 64
HEAD_DIM = 128


def expand(weight, mask):
    rows_in, cols_in = weight.shape
    tiles = weight.reshape(rows_in // BLOCK, BLOCK, cols_in // BLOCK, BLOCK)
    tiles = tiles * mask.astype(weight.dtype)[:, None, :, None]
    return tiles.reshape(rows_in, cols_in)


def activate(value):
    return jax.nn.gelu(value, approximate=True)


def times_transposed(left, right):
    return lax.dot_general(
        left, right, (((1,), (1,)), ((), ())), preferred_element_type=jnp.float32
    )


def over_tokens(left, right):
    return lax.dot_general(
        left, right, (((0,), (0,)), ((), ())), preferred_element_type=jnp.float32
    )


def body(tokens, up_weight, up_mask, down_weight, down_mask, grad_out):
    w_up = expand(up_weight, up_mask)
    w_down = expand(down_weight, down_mask)
    tok_all = lax.all_gather(tokens, "col", axis=0, tiled=True)
    token_count = tok_all.shape[0]
    col_share = token_count // lax.axis_size("col")
    piece = tok_all
    pre_act = lax.psum_scatter(
        jnp.dot(piece, w_up, preferred_element_type=jnp.float32).astype(jnp.bfloat16),
        "row",
        scatter_dimension=0,
        tiled=True,
    ).astype(jnp.float32)
    hidden = activate(pre_act).astype(jnp.bfloat16)
    hidden_all = lax.all_gather(hidden, "row", axis=0, tiled=True)
    piece = hidden_all
    output_rows = lax.psum_scatter(
        jnp.dot(piece, w_down, preferred_element_type=jnp.float32).astype(jnp.bfloat16),
        "col",
        scatter_dimension=0,
        tiled=True,
    )
    out_heads = output_rows.reshape(
        col_share, output_rows.shape[1] // HEAD_DIM, HEAD_DIM
    ).transpose(1, 0, 2)
    cot_all = lax.all_gather(grad_out, "col", axis=0, tiled=True)
    piece = cot_all
    grad_hidden = lax.psum_scatter(
        times_transposed(piece, w_down).astype(jnp.bfloat16), "row", scatter_dimension=0, tiled=True
    ).astype(jnp.float32)
    unused, pull = jax.vjp(activate, pre_act)
    grad_pre = pull(grad_hidden)[0].astype(jnp.bfloat16)
    grad_pre_all = lax.all_gather(grad_pre, "row", axis=0, tiled=True)
    grad_scale = 1.0 / math.sqrt(token_count)
    grad_up = expand(over_tokens(tok_all, grad_pre_all) * grad_scale, up_mask).astype(jnp.bfloat16)
    grad_down = expand(over_tokens(hidden_all, cot_all) * grad_scale, down_mask).astype(
        jnp.bfloat16
    )
    piece = grad_pre_all
    grad_tokens = lax.psum_scatter(
        times_transposed(piece, w_up).astype(jnp.bfloat16), "col", scatter_dimension=0, tiled=True
    )
    return (out_heads, grad_tokens, grad_up, grad_down)


def solution(mesh):
    return jax.shard_map(
        body,
        mesh=mesh,
        in_specs=(
            P("col", "row"),
            P("row", "col"),
            P("row", "col"),
            P("col", "row"),
            P("col", "row"),
            P("col", "row"),
        ),
        out_specs=(P("row", "col", None), P("col", "row"), P("row", "col"), P("col", "row")),
        check_vma=False,
    )
```

profile of v0, /device:TPU:1, one launch (start us, length us, event | category | flops | bytes accessed | tf_op | source)
XLA Modules:
  0.0 610.1 jit_solution(4705997597800748975)
XLA Ops:
  9.5 12.7 %mul.107 = bf16[48,64,48,64]{3,2,1,0:T(8,128)(2,1)} broadcast(bf16[48,48]{1,0:T(8,128)(2,1)S(1)} %get-tuple-element.15), dimensions={0,2} | broadcast | bytes 18878976 | tf_op jit(solution)/shard_map/mul | solution.py:15
  22.2 46.9 %mul.108 = bf16[3072,3072]{1,0:T(8,128)(2,1)} reshape(bf16[48,64,48,64]{3,2,1,0:T(8,128)(2,1)} %mul.107) | data formatting | bytes 37748736 | tf_op jit(solution)/shard_map/mul | solution.py:15
  69.1 18.0 %fusion.12 = bf16[512,3072]{0,1:T(8,128)(2,1)S(1)} fusion(bf16[512,3072]{1,0:T(8,128)(2,1)} %all-gather.9.cloned.1.call-done, bf16[3072,3072]{1,0:T(8,128)(2,1)} %param.9, bf16[3072,3072]{1,0:T(8,128)(2,1)} %mul.108), kind=kOutput, calls=%fused_computation.12 | convolution fusion | flops 9674686464 | bytes 44040192 | tf_op jit(solution)/shard_map/dot_general | solution.py:24
  87.2 3.0 copy.18
  90.9 12.6 %mul.100 = bf16[48,64,48,64]{3,2,1,0:T(8,128)(2,1)} broadcast(bf16[48,48]{1,0:T(8,128)(2,1)S(1)} %get-tuple-element.17), dimensions={0,2} | broadcast | bytes 18878976 | tf_op jit(solution)/shard_map/mul | solution.py:15
  103.6 46.7 %mul.101 = bf16[3072,3072]{1,0:T(8,128)(2,1)} reshape(bf16[48,64,48,64]{3,2,1,0:T(8,128)(2,1)} %mul.100) | data formatting | bytes 37748736 | tf_op jit(solution)/shard_map/mul | solution.py:15
  150.2 23.7 %mul.102 = bf16[3072,3072]{1,0:T(8,128)(2,1)} multiply(bf16[3072,3072]{1,0:T(8,128)(2,1)} %param.7, bf16[3072,3072]{1,0:T(8,128)(2,1)} %mul.101) | non-fusion elementwise | flops 9437184 | bytes 56623104 | tf_op jit(solution)/shard_map/mul | solution.py:15
  174.0 14.9 %fusion.11 = bf16[512,3072]{0,1:T(8,128)(2,1)S(1)} fusion(bf16[3072,3072]{1,0:T(8,128)(2,1)} %mul.102, bf16[512,3072]{1,0:T(8,128)(2,1)} %all-gather.5.cloned.1.call-done), kind=kOutput, calls=%fused_computation.11 | convolution fusion | flops 9665249280 | bytes 25165824 | tf_op jit(solution)/shard_map/dot_general | solution.py:43
  188.8 3.1 copy.16
  192.0 1.5 copy.19
  193.5 60.5 %reduce-scatter.13.cloned.1.call-done = bf16[128,3072]{1,0:T(8,128)(2,1)} async-done(((bf16[512,3072]{1,0:T(8,128)(2,1)}), bf16[128,3072]{1,0:T(8,128)(2,1)}) %reduce-scatter.13.cloned.1.call-update) | async-done | bytes 786448
  255.5 2.4 fusion.18
  258.8 63.0 %all-gather.7.cloned.1.call-done = bf16[512,3072]{0,1:T(8,128)(2,1)} async-done(((bf16[128,3072]{0,1:T(8,128)(2,1)}), bf16[512,3072]{0,1:T(8,128)(2,1)}) %all-gather.7.cloned.1.call-update) | async-done | bytes 3145744 | tf_op jit(solution)/shard_map/all_gather | solution.py:49
  321.9 19.7 %fusion.8 = bf16[512,3072]{1,0:T(8,128)(2,1)} fusion(bf16[512,3072]{0,1:T(8,128)(2,1)} %all-gather.7.cloned.1.call-done, bf16[3072,3072]{1,0:T(8,128)(2,1)} %param.9, bf16[3072,3072]{1,0:T(8,128)(2,1)} %mul.108), kind=kOutput, calls=%fused_computation.9 | convolution fusion | flops 9674686464 | bytes 44040192 | tf_op jit(solution)/shard_map/dot_general | solution.py:52
  341.8 23.9 %mul.127 = f32[48,64,48,64]{3,2,1,0:T(8,128)} broadcast(f32[48,48]{1,0:T(8,128)S(1)} %get-tuple-element.14), dimensions={0,2} | broadcast | bytes 37757952 | tf_op jit(solution)/shard_map/mul | solution.py:15
  365.7 60.1 %mul.128 = f32[3072,3072]{1,0:T(8,128)} reshape(f32[48,64,48,64]{3,2,1,0:T(8,128)} %mul.127) | data formatting | bytes 75497472 | tf_op jit(solution)/shard_map/mul | solution.py:15
  425.8 23.7 %mul.123 = f32[48,64,48,64]{1,0,3,2:T(8,128)} broadcast(f32[48,48]{0,1:T(8,128)S(1)} %copy.14), dimensions={0,2} | broadcast | bytes 37757952 | tf_op jit(solution)/shard_map/mul | solution.py:15
  449.5 59.5 %mul.124 = f32[3072,3072]{0,1:T(8,128)} reshape(f32[48,64,48,64]{1,0,3,2:T(8,128)} %mul.123) | data formatting | bytes 75497472 | tf_op jit(solution)/shard_map/mul | solution.py:15
  509.0 15.9 %convolution_convert_fusion = bf16[512,3072]{1,0:T(8,128)(2,1)} fusion(bf16[512,3072]{0,1:T(8,128)(2,1)} %all-gather.11.cloned.1.call-done, bf16[3072,3072]{1,0:T(8,128)(2,1)} %mul.102), kind=kOutput, calls=%fused_computation.8 | convolution fusion | flops 9665249280 | bytes 25165824 | tf_op jit(solution)/shard_map/dot_general | solution.py:24
  525.0 1.9 copy-done.1
  526.8 25.5 %fusion = bf16[3072,3072]{0,1:T(8,128)(2,1)} fusion(f32[3072,3072]{0,1:T(8,128)} %mul.124, bf16[512,3072]{0,1:T(8,128)(2,1)S(1)} %copy-done.1, bf16[512,3072]{1,0:T(8,128)(2,1)} %all-gather.5.cloned.1.call-done), kind=kOutput, calls=%fused_computation.1 | convolution fusion | flops 9691987968 | bytes 62914560 | tf_op jit(solution)/shard_map/dot_general | solution.py:30
  552.3 24.8 %copy.15 = bf16[3072,3072]{1,0:T(8,128)(2,1)} copy(bf16[3072,3072]{0,1:T(8,128)(2,1)} %fusion) | data formatting | bytes 37748736
  577.1 24.3 %multiply_convert_fusion = bf16[3072,3072]{1,0:T(8,128)(2,1)} fusion(f32[3072,3072]{1,0:T(8,128)} %mul.128, bf16[512,3072]{0,1:T(8,128)(2,1)S(1)} %copy-done, bf16[512,3072]{1,0:T(8,128)(2,1)} %all-gather.9.cloned.1.call-done), kind=kOutput, calls=%fused_computation.2 | convolution fusion | flops 9691987968 | bytes 62914560 | tf_op jit(solution)/shard_map/dot_general | solution.py:30
  601.4 1.9 bitcast_bitcast_fusion
  (31 shorter events, 5.6 us)
Async XLA Ops:
  7.2 62.0 %all-gather.9.cloned.1.call-start = ((), (), s32[]{:S(2)}) async-start(), calls=%async_computation.7 | async-start | bytes 3538944 | tf_op jit(solution)/shard_map/all_gather | solution.py:60
  7.9 166.1 %all-gather.5.cloned.1.call-start = ((), (), s32[]{:S(2)}) async-start(), calls=%async_computation.4 | async-start | bytes 3538944 | tf_op jit(solution)/shard_map/all_gather | solution.py:38
  8.6 183.3 %reduce-scatter.15.cloned.1.call-start = ((), (), s32[]{:S(2)}) async-start(), calls=%async_computation.11 | async-start | bytes 3932160
  90.2 0.7 copy-start.2
  90.2 163.8 %reduce-scatter.13.cloned.1.call-start = ((), (), s32[]{:S(2)}) async-start(), calls=%async_computation.10 | async-start | bytes 3932160
  191.9 130.0 %all-gather.7.cloned.1.call-start = ((), (), s32[]{:S(2)}) async-start(), calls=%async_computation.5 | async-start | bytes 3932160 | tf_op jit(solution)/shard_map/all_gather | solution.py:49
  258.0 251.0 %all-gather.11.cloned.1.call-start = ((), (), s32[]{:S(2)}) async-start(), calls=%async_computation.8 | async-start | bytes 3932160 | tf_op jit(solution)/shard_map/all_gather | solution.py:67
  258.6 342.8 %reduce-scatter.9.cloned.1.call-start = ((), (), s32[]{:S(2)}) async-start(), calls=%async_computation.6 | async-start | bytes 3538944 | tf_op jit(solution)/shard_map/reduce_scatter | solution.py:51
  341.6 261.6 %reduce-scatter.11.cloned.1.call-start = ((), (), s32[]{:S(2)}) async-start(), calls=%async_computation.9 | async-start | bytes 3538944 | tf_op jit(solution)/shard_map/reduce_scatter | solution.py:74
  524.9 1.9 copy-start.1
  552.3 24.8 %copy-start = (bf16[512,3072]{0,1:T(8,128)(2,1)S(1)}, bf16[512,3072]{0,1:T(8,128)(2,1)}, u32[]{:S(2)}) copy-start(bf16[512,3072]{0,1:T(8,128)(2,1)} %all-gather.7.cloned.1.call-done) | copy-start | bytes 9437188
Sparse Core Ops, SparseCore 0:
  9.9 34.8 all-gather.8
  46.6 32.3 all-gather.4
  90.3 61.9 reduce-scatter.14
  192.0 61.9 reduce-scatter.12
  258.1 63.7 all-gather.6
  323.3 61.5 all-gather.10
  388.3 44.2 reduce-scatter.8
  525.1 44.2 reduce-scatter.10
where the time goes:
time: 616 us; the launch traced here: 610 us
  local copies, waits for them, and re-layouts  324 us (53%)
  waiting for transfers between devices  126 us (20%)
  matrix products  118 us (19%)
  other arithmetic  27 us (4%)
  between operations  14.2 us (2%)
    mul x8, local copies, waits for them, and re-layouts, expand(): tiles = tiles * mask.astype(weight.dtype)[:, None, :, None]  286 us
    all_gather x1, waiting for transfers between devices, body(): hidden_all = lax.all_gather(hidden, 'row', axis=0, tiled=True)  63 us
    unnamed x10, waiting for transfers between devices  62.5 us
    dot_general x2, matrix products, over_tokens(): lax.dot_general(left, right, (((0,), (0,)), ((), ())), preferred_element_...  49.8 us
    unnamed x11, local copies, waits for them, and re-layouts  36.2 us
    dot_general x2, matrix products, times_transposed(): lax.dot_general(left, right, (((1,), (1,)), ((), ())), preferred_element_...  34 us
    mul x1, other arithmetic, expand(): tiles = tiles * mask.astype(weight.dtype)[:, None, :, None]  23.7 us
    dot_general x1, matrix products, body(): jnp.dot(piece, w_down, preferred_element_type=jnp.float32)  19.7 us
  transfers between devices with their start and end apart: 8, of which 2 were waited for; matrix products, arithmetic and copies ran while one was open for 76% of the time, Pallas kernels for 0%

commit v1 on v0

v1 whole, which is shorter than its diff:
```python
import functools
import math

import jax
import jax.numpy as jnp
from jax import lax
from jax.experimental import pallas as pl
from jax.experimental.pallas import tpu as pltpu
from jax.sharding import PartitionSpec as P

BLOCK = 64
HEAD_DIM = 128
TILE = 512
ROW_STEP = 16
VMEM_LIMIT = 40 * 1024 * 1024
GELU_A = 0.7978845608
GELU_B = 0.044715


def lane_mask(mask_rows, width, first_block):
    blocks = mask_rows.shape[1]
    block = lax.broadcasted_iota(jnp.int32, (blocks, width), 0)
    column = lax.broadcasted_iota(jnp.int32, (blocks, width), 1)
    pick = (column // BLOCK + first_block == block).astype(jnp.float32)
    return jnp.dot(mask_rows.astype(jnp.float32), pick, preferred_element_type=jnp.float32)


def stack_into(scratch, refs):
    at = 0
    for ref in refs:
        scratch[at : at + ref.shape[0], :] = ref[...]
        at += ref.shape[0]


def weight_kernel(n_in, n_out, transposed, x_refs, tail, out_refs, scratch):
    w_ref, mask_ref = tail
    x_all, w_kept = scratch
    step = pl.program_id(0)

    @pl.when(step == 0)
    def _():
        stack_into(x_all, x_refs)

    depth, width = w_ref.shape
    if transposed:
        blocks = depth // BLOCK
        mask_rows = mask_ref[pl.ds(pl.multiple_of(step * blocks, blocks), blocks), :]
        kept = lane_mask(mask_rows, width, 0)
    else:
        kept = lane_mask(mask_ref[...], width, step * (width // BLOCK))
    kept = kept.astype(jnp.bfloat16)
    for block in range(depth // BLOCK):
        rows = slice(block * BLOCK, (block + 1) * BLOCK)
        w_kept[rows, :] = w_ref[rows, :] * kept[block : block + 1, :]
    contract = ((1,), (1,)) if transposed else ((1,), (0,))
    product = lax.dot_general(
        x_all[...], w_kept[...], (contract, ((), ())), preferred_element_type=jnp.float32
    )
    at = 0
    for out_ref in out_refs:
        out_ref[...] = product[at : at + out_ref.shape[0], :].astype(out_ref.dtype)
        at += out_ref.shape[0]


def grad_kernel(n_x, scale, refs, tail, out_refs, scratch):
    x_refs, g_refs = refs[:n_x], refs[n_x:]
    (mask_ref,), (out_ref,), (x_all, g_all) = tail, out_refs, scratch
    step = pl.program_id(0)

    @pl.when(step == 0)
    def _():
        stack_into(g_all, g_refs)

    stack_into(x_all, x_refs)
    depth, width = out_ref.shape
    blocks = depth // BLOCK
    mask_rows = mask_ref[pl.ds(pl.multiple_of(step * blocks, blocks), blocks), :]
    kept = lane_mask(mask_rows, width, 0) * scale
    product = lax.dot_general(
        x_all[...], g_all[...], (((0,), (0,)), ((), ())), preferred_element_type=jnp.float32
    )
    for block in range(blocks):
        rows = slice(block * BLOCK, (block + 1) * BLOCK)
        out_ref[rows, :] = (product[rows, :] * kept[block : block + 1, :]).astype(out_ref.dtype)


def gelu_and_slope(value):
    square = value * value
    tanh = jnp.tanh(GELU_A * (value + GELU_B * (value * square)))
    half = 0.5 * (1.0 + tanh)
    slope = half + 0.5 * value * (1.0 - tanh * tanh) * (GELU_A * (1.0 + (3.0 * GELU_B) * square))
    return value * half, slope


def sum_kernel(finish, n_sum, refs, tail, out_refs, scratch):
    @pl.loop(0, refs[0].shape[0] // ROW_STEP)
    def _(step):
        rows = pl.ds(pl.multiple_of(step * ROW_STEP, ROW_STEP), ROW_STEP)
        width = refs[0].shape[1]
        for first in range(0, width, TILE):
            columns = slice(first, first + TILE)
            values = [ref[rows, columns].astype(jnp.float32) for ref in refs]
            total = values[0]
            for value in values[1:n_sum]:
                total = total + value
            for out_ref, result in zip(out_refs, finish(total, *values[n_sum:])):
                out_ref[rows, columns] = result.astype(out_ref.dtype)


def dispatch(kernel, counts, *refs):
    n_pieces, n_tail, n_pass, n_after, n_out = counts
    refs = refs[1:]
    tail = refs[n_pieces : n_pieces + n_tail]
    outs = refs[n_pieces + n_tail + n_pass + n_after :]
    kernel(refs[:n_pieces], tail, outs[:n_out], outs[n_out + n_pass :])


class Order:
    def __init__(self, place):
        self.place = place
        self.last = None

    def call(self, kernel, grid, pieces, piece_specs, tail, tail_specs, outs, out_specs, scratch, passing):
        after = [] if self.last is None else [self.last]
        operands = list(pieces) + list(tail) + list(passing) + after
        anywhere = pl.BlockSpec(memory_space=pl.ANY)
        first_pass = 1 + len(pieces) + len(tail)
        results = pl.pallas_call(
            functools.partial(
                dispatch, kernel, (len(pieces), len(tail), len(passing), len(after), len(outs))
            ),
            grid_spec=pltpu.PrefetchScalarGridSpec(
                num_scalar_prefetch=1,
                grid=grid,
                in_specs=list(piece_specs) + list(tail_specs) + [anywhere] * (len(passing) + len(after)),
                out_specs=list(out_specs) + [anywhere] * len(passing),
                scratch_shapes=scratch,
            ),
            out_shape=list(outs) + [jax.ShapeDtypeStruct(p.shape, p.dtype) for p in passing],
            input_output_aliases={first_pass + i: len(outs) + i for i in range(len(passing))},
            compiler_params=pltpu.CompilerParams(vmem_limit_bytes=VMEM_LIMIT),
            cost_estimate=pl.CostEstimate(flops=1, bytes_accessed=1, transcendentals=0),
        )(self.place, *operands)
        self.last = results[0]
        return list(results)

    def piece(self, piece, width, column):
        if isinstance(piece, tuple):
            array, k = piece
            rows = array.shape[0] // self.place.shape[0]
            return array, rows, pl.BlockSpec((rows, width), lambda j, place: (place[k], column(j)))
        return piece, piece.shape[0], pl.BlockSpec((piece.shape[0], width), lambda j, place: (0, column(j)))

    def times_weight(self, pieces, weight, mask, splits, transposed, passing=(), tile=TILE):
        depth, width = weight.shape
        x_width, out_width = (width, depth) if transposed else (depth, width)
        arrays, rows, specs = zip(*[self.piece(p, x_width, lambda j: 0) for p in pieces])
        w_block = (tile, width) if transposed else (depth, tile)
        w_map = (lambda j, place: (j, 0)) if transposed else (lambda j, place: (0, j))
        return self.call(
            functools.partial(weight_kernel, len(pieces), len(splits), transposed),
            (out_width // tile,),
            arrays,
            specs,
            [weight, mask],
            [pl.BlockSpec(w_block, w_map), pl.BlockSpec(mask.shape, lambda j, place: (0, 0))],
            [jax.ShapeDtypeStruct((split, out_width), jnp.bfloat16) for split in splits],
            [pl.BlockSpec((split, tile), lambda j, place: (0, j)) for split in splits],
            [pltpu.VMEM((sum(rows), x_width), jnp.bfloat16), pltpu.VMEM(w_block, jnp.bfloat16)],
            passing,
        )

    def weight_grad(self, x_pieces, g_pieces, mask, depth, width, scale, passing=(), tile=TILE):
        x_arrays, x_rows, x_specs = zip(*[self.piece(p, tile, lambda j: j) for p in x_pieces])
        g_arrays, g_rows, g_specs = zip(*[self.piece(p, width, lambda j: 0) for p in g_pieces])
        return self.call(
            functools.partial(grad_kernel, len(x_pieces), scale),
            (depth // tile,),
            x_arrays + g_arrays,
            x_specs + g_specs,
            [mask],
            [pl.BlockSpec(mask.shape, lambda j, place: (0, 0))],
            [jax.ShapeDtypeStruct((depth, width), jnp.bfloat16)],
            [pl.BlockSpec((tile, width), lambda j, place: (j, 0))],
            [pltpu.VMEM((sum(x_rows), tile), jnp.bfloat16), pltpu.VMEM((sum(g_rows), width), jnp.bfloat16)],
            passing,
        )

    def summed(self, finish, arrays, others, n_out, passing=()):
        shape = arrays[0].shape
        whole = pl.BlockSpec(shape, lambda j, place: (0, 0))
        operands = list(arrays) + list(others)
        return self.call(
            functools.partial(sum_kernel, finish, len(arrays)),
            (1,),
            operands,
            [whole] * len(operands),
            [],
            [],
            [jax.ShapeDtypeStruct(shape, jnp.bfloat16)] * n_out,
            [whole] * n_out,
            [],
            passing,
        )


def only_sum(total):
    return (total,)


class Chain:
    def __init__(self, order, n_row):
        self.order, self.n_row, self.got = order, n_row, []

    def send(self, value):
        hop = len(self.got)
        pairs = [(hop, hop + 1), (self.n_row - 1 - hop, self.n_row - 2 - hop)]
        self.got.append(lax.ppermute(value, "row", pairs))

    def start(self, part):
        self.part = part
        self.send(part)

    def advance(self, passing=()):
        total, *passed = self.order.summed(only_sum, [self.part, self.got[-1]], [], 1, passing)
        self.send(total)
        return passed

    def total(self, finish, others, n_out, passing=()):
        return self.order.summed(finish, [self.part] + self.got, others, n_out, passing)


def body(tokens, up_weight, up_mask, down_weight, down_mask, grad_out):
    n_row, n_col = lax.axis_size("row"), lax.axis_size("col")
    share, model = tokens.shape
    hidden_units = up_weight.shape[1]
    grad_scale = 1.0 / math.sqrt(share * n_col)
    chips = n_col // 2
    place = lax.axis_index("col") ^ jnp.arange(n_col, dtype=jnp.int32)
    order = Order(place)

    def swap(value, offset):
        return lax.ppermute(value, "col", [(i, i ^ offset) for i in range(n_col)])

    tok = [tokens, swap(tokens, 1)] + [None] * (n_col - 2)
    cot_partner = swap(grad_out, 1)
    for offset in range(2, n_col, 2):
        tok[offset] = swap(tokens, offset)
    for offset in range(2, n_col, 2):
        tok[offset + 1] = swap(tok[offset], 1)
    cot_all = lax.all_gather(grad_out, "col", axis=0, tiled=True)
    cot = [grad_out, cot_partner] + [(cot_all, k) for k in range(2, n_col)]

    sizes = [share, share] + [2 * share] * (chips - 1)
    n_chunk = len(sizes)
    queue = [("a", 0), ("a", 1), ("b", 1), ("a", 2), ("a", 3), ("b", 2)]
    for chunk in range(4, n_chunk):
        queue += [("a", chunk), ("b", chunk - 1)]
    queue += [("b", n_chunk - 1), ("b", 0)]
    parts, chains = {}, {}
    hidden, slope, grad_pre = {}, {}, {}
    for key in queue:
        chains[key] = Chain(order, n_row)

    def pass_next(kernel, key):
        if key is None:
            return kernel(())
        *results, part = kernel((parts[key],))
        chains[key].start(part)
        return results

    def finish(key, passing=()):
        kind, chunk = key
        if kind == "a":
            hidden[chunk], slope[chunk], *passed = chains[key].total(gelu_and_slope, [], 2, passing)
        else:
            grad_pre[chunk], *passed = chains[key].total(lambda total, rise: (total * rise,), [slope[chunk]], 1, passing)
        return passed

    def pre(chunks, passing=()):
        pieces, splits = [], []
        for chunk in chunks:
            pieces += [tok[chunk]] if chunk < 2 else tok[2 * chunk - 2 : 2 * chunk]
            splits.append(sizes[chunk])
        results = order.times_weight(pieces, up_weight, up_mask, splits, False, passing)
        for chunk, result in zip(chunks, results):
            parts["a", chunk] = result
        return results[len(chunks) :]

    def back(chunks, passing=()):
        pieces, splits = [], []
        for chunk in chunks:
            pieces += [cot[chunk]] if chunk < 2 else cot[2 * chunk - 2 : 2 * chunk]
            splits.append(sizes[chunk])
        results = order.times_weight(pieces, down_weight, down_mask, splits, True, passing)
        for chunk, result in zip(chunks, results):
            parts["b", chunk] = result
        return results[len(chunks) :]

    def up_back(chunks, passing=()):
        splits = []
        for chunk in chunks:
            splits += [share] if chunk < 2 else [share, share]
        return order.times_weight([grad_pre[chunk] for chunk in chunks], up_weight, up_mask, splits, True, passing)

    def pair_sum(keep, give):
        return order.summed(only_sum, [keep, swap(give, 1)], [], 1)[0]

    tok_parts, out_got, tok_got = [None] * n_col, [], []
    results = {}

    def work_out(passing):
        out, *rest = [order.times_weight([hidden[c] for c in range(n_chunk)], down_weight, down_mask, [share] * n_col, False, passing)], ()
        outs = out[0]
        results["out"] = outs[:n_col]
        return outs[n_col:]

    def work_down(passing):
        down, *passed = order.weight_grad(
            [hidden[c] for c in range(n_chunk)], cot, down_mask, hidden_units, model, grad_scale, passing
        )
        results["down"] = down
        return passed

    def work_tok(chunks):
        def run(passing):
            outs = up_back(chunks, passing)
            at = 0
            for chunk in chunks:
                first = chunk if chunk < 2 else 2 * chunk - 2
                count = 1 if chunk < 2 else 2
                tok_parts[first : first + count] = outs[at : at + count]
                at += count
            return outs[at:]

        return run

    total_slots = len(queue) + n_row - 2
    work = {slot: [] for slot in range(total_slots + 1)}
    place_of = {key: i for i, key in enumerate(queue)}
    work[0] = [lambda passing: pre([2, 3], passing)]
    work[2] = [lambda passing: pre(list(range(4, n_chunk)), passing)]
    work[3] = [lambda passing: back(list(range(2, n_chunk)) + [0], passing)]

    def ready(key):
        return place_of[key] + n_row - 2

    last_a = ready(("a", n_chunk - 1))
    work[last_a].append(work_out)
    work[last_a + 1].append(work_down)
    held = []
    for chunk in range(2, n_chunk):
        slot = ready(("b", chunk))
        if slot == last_a + 1:
            held.append(chunk)
        else:
            work[slot].append(work_tok(held + [chunk]))
            held = []

    pre([0])
    chains[queue[0]].start(parts[queue[0]])
    pre([1])
    chains[queue[1]].start(parts[queue[1]])
    back([1])
    chains[queue[2]].start(parts[queue[2]])
    started = 3
    for slot in range(total_slots + 1):
        for hop in range(n_row - 1):
            at = slot - hop
            if 0 <= at < len(queue):
                if hop < n_row - 2:
                    chains[queue[at]].advance()
                else:
                    finish(queue[at])
        todo = work.get(slot, [])
        for index, step in enumerate(todo):
            key = None
            if index == len(todo) - 1 and slot >= 1 and started < len(queue):
                key = queue[started]
                if key not in parts:
                    step(())
                    chains[key].start(parts[key])
                else:
                    pass_next(step, key)
                started += 1
            else:
                step(())
        if not todo and slot >= 1 and started < len(queue):
            key = queue[started]
            chains[key].start(parts[key])
            started += 1

    work_tok([1])(())
    work_tok([0])(())
    up = order.weight_grad(tok, [grad_pre[c] for c in range(n_chunk)], up_mask, model, hidden_units, grad_scale)

    def over_col(parts_of):
        total = parts_of[0].astype(jnp.float32) + swap(parts_of[1], 1).astype(jnp.float32)
        for offset in range(2, n_col, 2):
            give = swap(parts_of[offset + 1], 1).astype(jnp.float32)
            both = (parts_of[offset].astype(jnp.float32) + give).astype(jnp.bfloat16)
            total = total + swap(both, offset).astype(jnp.float32)
        return total.astype(jnp.bfloat16)

    output_rows = over_col(results["out"])
    grad_tokens = over_col(tok_parts)
    out_heads = output_rows.reshape(share, model // HEAD_DIM, HEAD_DIM).transpose(1, 0, 2)
    return (out_heads, grad_tokens, up[0], results["down"])


def solution(mesh):
    return jax.shard_map(
        body,
        mesh=mesh,
        in_specs=(
            P("col", "row"),
            P("row", "col"),
            P("row", "col"),
            P("col", "row"),
            P("col", "row"),
            P("col", "row"),
        ),
        out_specs=(P("row", "col", None), P("col", "row"), P("row", "col"), P("col", "row")),
        check_vma=False,
    )
```

time: 616 us -> 344 us (0.56)
  local copies, waits for them, and re-layouts: 324 us -> 5.09 us
  Pallas kernels: 0 us -> 191 us
  matrix products: 118 us -> 0 us
  waiting for transfers between devices: 126 us -> 31.3 us
  starting transfers between devices: 0.72 us -> 93 us
  other arithmetic: 27 us -> 5.34 us
    mul x8 -> x0, local copies, waits for them, and re-layouts: 286 us -> none  [expand(): tiles = tiles * mask.astype(weight.dtype)[:, None, :, None]]
    pallas_call x0 -> x43, Pallas kernels: none -> 191 us  [call(): pl.pallas_call(functools.partial(dispatch, kernel, (len(pieces), len(tail...]
    dot_general x6 -> x0, matrix products: 118 us -> none  [the longest x2 49.8 us: over_tokens(): lax.dot_general(left, right, (((0,), (0,)), ((), ())), preferred_element_...]
    ppermute x0 -> x52, starting transfers between devices: none -> 93 us  [the longest x30 68.3 us: send(): self.got.append(lax.ppermute(value, 'row', pairs))]
    all_gather x3 -> x0, waiting for transfers between devices: 63.1 us -> none  [the longest x1 63 us: body(): hidden_all = lax.all_gather(hidden, 'row', axis=0, tiled=True)]
    unnamed x10 -> x1, waiting for transfers between devices: 62.5 us -> 0.68 us
    unnamed x11 -> x82, local copies, waits for them, and re-layouts: 36.2 us -> 5.09 us
    ppermute x0 -> x52, waiting for transfers between devices: none -> 30.6 us  [the longest x30 29 us: send(): self.got.append(lax.ppermute(value, 'row', pairs))]
  transfers between devices with their start and end apart: 8 -> 53, of which waited for: 2 -> 8; matrix products, arithmetic and copies ran while one was open for 76% -> 1% of each run, Pallas kernels for 0% -> 56%
where the time goes in v1:
time: 344 us; the launch traced here: 341 us
  Pallas kernels  191 us (56%)
  starting transfers between devices  93 us (27%)
  waiting for transfers between devices  31.3 us (9%)
  between operations  15.2 us (4%)
  other arithmetic  5.34 us (2%)
  local copies, waits for them, and re-layouts  5.09 us (1%)
    pallas_call x43, Pallas kernels, call(): pl.pallas_call(functools.partial(dispatch, kernel, (len(pieces), len(tail...  191 us
    ppermute x30, starting transfers between devices, send(): self.got.append(lax.ppermute(value, 'row', pairs))  68.3 us
    ppermute x30, waiting for transfers between devices, send(): self.got.append(lax.ppermute(value, 'row', pairs))  29 us
    ppermute x22, starting transfers between devices, swap(): return lax.ppermute(value, 'col', [(i, i ^ offset) for i in range(n_col)])  24.7 us
  transfers between devices with their start and end apart: 53, of which 8 were waited for; matrix products, arithmetic and copies ran while one was open for 1% of the time, Pallas kernels for 56%

profile of v1, /device:TPU:1, one launch (start us, length us, event | category | flops | bytes accessed | tf_op | source)
XLA Modules:
  0.0 341.1 jit_solution(6969037283876627116)
XLA Ops:
  13.2 10.4 %shard_map.93.refs_4_.refs_1_ = bf16[64,3072]{1,0:T(8,128)(2,1)S(1)} custom-call(s32[8]{0:T(128)S(1)} %iota_xor_fusion.refs_0_, bf16[64,3072]{1,0:T(8,128)(2,1)} %refs_1_.3, bf16[3072,3072]{1,0:T(8,128)(2,1)} %refs_2_.11, s32[48,48]{1,0:T(8,128)S(1)} %copy-done.7), custom_call_target="tpu_custom_call" | custom-call | flops 1 | bytes 1 | tf_op jit(solution)/shard_map/pallas_call | solution.py:128
  23.6 3.2 collective-permute-start
  27.8 10.6 %shard_map.94.refs_4_.refs_1_ = bf16[64,3072]{1,0:T(8,128)(2,1)S(1)} custom-call(s32[8]{0:T(128)S(1)} %iota_xor_fusion.refs_0_, bf16[64,3072]{1,0:T(8,128)(2,1)S(1)} %collective-permute-done.2.refs_1_.refs_2_, bf16[3072,3072]{1,0:T(8,128)(2,1)} %refs_2_.11, s32[48,48]{1,0:T(8,128)S(1)} %copy-done.7, bf16[64,3072]{1,0:T(8,128)(2,1)S(1)} %shard_map.93.refs_4_.refs_1_), custom_call_target="tpu_custom_call" | custom-call | flops 1 | bytes 1 | tf_op jit(solution)/shard_map/pallas_call | solution.py:128
  39.8 11.5 %shard_map.95.refs_3_.refs_1_ = bf16[64,3072]{1,0:T(8,128)(2,1)S(1)} custom-call(s32[8]{0:T(128)S(1)} %iota_xor_fusion.refs_0_, bf16[64,3072]{1,0:T(8,128)(2,1)S(1)} %collective-permute-done.1.refs_1_.refs_7_, bf16[3072,3072]{1,0:T(8,128)(2,1)} %refs_6_.4, s32[48,48]{1,0:T(8,128)S(1)} %copy-done.38, bf16[64,3072]{1,0:T(8,128)(2,1)S(1)} %shard_map.94.refs_4_.refs_1_), custom_call_target="tpu_custom_call" | custom-call | flops 1 | bytes 1 | tf_op jit(solution)/shard_map/pallas_call | solution.py:128
  52.8 11.3 %shard_map.97 = (bf16[128,3072]{1,0:T(8,128)(2,1)S(1)}, bf16[128,3072]{1,0:T(8,128)(2,1)S(1)}) custom-call(s32[8]{0:T(128)S(1)} %iota_xor_fusion.refs_0_, bf16[64,3072]{1,0:T(8,128)(2,1)S(1)} %collective-permute-done.5.refs_1_.refs_3_, bf16[64,3072]{1,0:T(8,128)(2,1)S(1)} %collective-permute-done.6.refs_2_.refs_4_, ...), custom_call_target="tpu_custom_call" | custom-call | flops 1 | bytes 1 | tf_op jit(solution)/shard_map/pallas_call | solution.py:128
  64.1 3.6 %collective-permute-start.14 = (bf16[128,3072]{1,0:T(8,128)(2,1)S(1)}, bf16[128,3072]{1,0:T(8,128)(2,1)S(1)}, u32[]{:S(2)}, u32[]{:S(2)}) collective-permute-start(bf16[128,3072]{1,0:T(8,128)(2,1)S(1)} %get-tuple-element.37.refs_3_.refs_1_), channel_id=1, source_target_pairs={{0,8},{24,16},{1,9},{25,17},{2,10},{26,18},{3,11},{27,19},{4,12},{... | collective-permute-start | bytes 2359304 | tf_op jit(solution)/shard_map/ppermute | solution.py:218
  73.7 18.1 %collective-permute-done.11.refs_2_ = bf16[64,3072]{1,0:T(8,128)(2,1)S(1)} collective-permute-done((bf16[64,3072]{1,0:T(8,128)(2,1)S(1)}, bf16[64,3072]{1,0:T(8,128)(2,1)S(1)}, u32[]{:S(2)}, u32[]{:S(2)}) %collective-permute-start.11) | collective-permute-done | bytes 393248 | tf_op jit(solution)/shard_map/ppermute | solution.py:218
  96.4 9.9 %shard_map.103 = (bf16[128,3072]{1,0:T(8,128)(2,1)S(1)}, bf16[128,3072]{1,0:T(8,128)(2,1)S(1)}) custom-call(s32[8]{0:T(128)S(1)} %iota_xor_fusion.refs_0_, bf16[64,3072]{1,0:T(8,128)(2,1)S(1)} %collective-permute-done.15.refs_1_.refs_7_, bf16[64,3072]{1,0:T(8,128)(2,1)S(1)} %collective-permute-done.16.refs_2_.refs_8_, ...), custom_call_target="tpu_custom_call", output_to_operand_aliasing={{1}: (5, {})} | custom-call | flops 1 | bytes 1 | tf_op jit(solution)/shard_map/pallas_call | solution.py:128
  106.4 6.5 %collective-permute-start.18 = (bf16[128,3072]{1,0:T(8,128)(2,1)S(1)}, bf16[128,3072]{1,0:T(8,128)(2,1)}, u32[]{:S(2)}, u32[]{:S(2)}) collective-permute-start(bf16[128,3072]{1,0:T(8,128)(2,1)S(1)} %get-tuple-element.42.refs_1_), channel_id=1, source_target_pairs={{0,8},{24,16},{1,9},{25,17},{2,10},{26,18},{3,11},{27,19},{4,12},{... | collective-permute-start | bytes 2359304 | tf_op jit(solution)/shard_map/ppermute | solution.py:218
  122.2 13.8 %shard_map.107 = (bf16[128,3072]{1,0:T(8,128)(2,1)S(1)}, bf16[128,3072]{1,0:T(8,128)(2,1)S(1)}, bf16[128,3072]{1,0:T(8,128)(2,1)S(1)}, bf16[64,3072]{1,0:T(8,128)(2,1)S(1)}) custom-call(s32[8]{0:T(128)S(1)} %iota_xor_fusion.refs_0_, bf16[512,3072]{1,0:T(8,128)(2,1)S(1)} %copy-done, bf16[512,3072]{1,0:T(8,128)(2,1)S(1)} %copy-done, ...), custom_call_target="tpu_custom_call" | custom-call | flops 1 | bytes 1 | tf_op jit(solution)/shard_map/pallas_call | solution.py:128
  145.3 5.8 %collective-permute-start.25 = (bf16[128,3072]{1,0:T(8,128)(2,1)S(1)}, bf16[128,3072]{1,0:T(8,128)(2,1)S(1)}, u32[]{:S(2)}, u32[]{:S(2)}) collective-permute-start(bf16[128,3072]{1,0:T(8,128)(2,1)S(1)} %get-tuple-element.40.refs_3_.refs_1_), channel_id=1, source_target_pairs={{0,8},{24,16},{1,9},{25,17},{2,10},{26,18},{3,11},{27,19},{4,12},{... | collective-permute-start | bytes 2359304 | tf_op jit(solution)/shard_map/ppermute | solution.py:218
  156.0 9.4 %collective-permute-start.27 = (bf16[128,3072]{1,0:T(8,128)(2,1)S(1)}, bf16[128,3072]{1,0:T(8,128)(2,1)S(1)}, u32[]{:S(2)}, u32[]{:S(2)}) collective-permute-start(bf16[128,3072]{1,0:T(8,128)(2,1)S(1)} %get-tuple-element.47.refs_1_), channel_id=1, source_target_pairs={{0,8},{24,16},{1,9},{25,17},{2,10},{26,18},{3,11},{27,19},{4,12},{... | collective-permute-start | bytes 2359304 | tf_op jit(solution)/shard_map/ppermute | solution.py:218
  172.8 9.4 %collective-permute-start.30 = (bf16[128,3072]{1,0:T(8,128)(2,1)S(1)}, bf16[128,3072]{1,0:T(8,128)(2,1)S(1)}, u32[]{:S(2)}, u32[]{:S(2)}) collective-permute-start(bf16[128,3072]{1,0:T(8,128)(2,1)S(1)} %get-tuple-element.48.refs_1_), channel_id=1, source_target_pairs={{0,8},{24,16},{1,9},{25,17},{2,10},{26,18},{3,11},{27,19},{4,12},{... | collective-permute-start | bytes 2359304 | tf_op jit(solution)/shard_map/ppermute | solution.py:218
  182.3 3.1 shard_map.116
  190.0 7.3 %collective-permute-done.31.refs_4_ = bf16[128,3072]{1,0:T(8,128)(2,1)S(1)} collective-permute-done((bf16[128,3072]{1,0:T(8,128)(2,1)S(1)}, bf16[128,3072]{1,0:T(8,128)(2,1)S(1)}, u32[]{:S(2)}, u32[]{:S(2)}) %collective-permute-start.31) | collective-permute-done | bytes 786464 | tf_op jit(solution)/shard_map/ppermute | solution.py:218
  198.4 11.8 %shard_map.120 = (bf16[64,3072]{1,0:T(8,128)(2,1)S(1)}, bf16[64,3072]{1,0:T(8,128)(2,1)S(1)}, bf16[64,3072]{1,0:T(8,128)(2,1)S(1)}) custom-call(s32[8]{0:T(128)S(1)} %iota_xor_fusion.refs_0_, bf16[128,3072]{1,0:T(8,128)(2,1)S(1)} %shard_map.119.refs_1_.refs_5_.refs_11_, bf16[3072,3072]{1,0:T(8,128)(2,1)} %refs_2_.11, ...), custom_call_target="tpu_custom_call", output_to_operand_aliasing={{2}: (4, {})} | custom-call | flops 1 | bytes 1 | tf_op jit(solution)/shard_map/pallas_call | solution.py:128
  211.7 4.1 %collective-permute-start.39 = (bf16[64,3072]{1,0:T(8,128)(2,1)S(1)}, bf16[64,3072]{1,0:T(8,128)(2,1)S(1)}, u32[]{:S(2)}, u32[]{:S(2)}) collective-permute-start(bf16[64,3072]{1,0:T(8,128)(2,1)S(1)} %get-tuple-element.61.refs_1_), channel_id=1, source_target_pairs={{0,8},{24,16},{1,9},{25,17},{2,10},{26,18},{3,11},{27,19},{4,12},{... | collective-permute-start | bytes 1179656 | tf_op jit(solution)/shard_map/ppermute | solution.py:218
  215.8 7.7 %collective-permute-start.46 = (bf16[64,3072]{1,0:T(8,128)(2,1)S(1)}, bf16[64,3072]{1,0:T(8,128)(2,1)S(1)}, u32[]{:S(2)}, u32[]{:S(2)}) collective-permute-start(bf16[64,3072]{1,0:T(8,128)(2,1)S(1)} %get-tuple-element.66), channel_id=1, source_target_pairs={{0,1},{1,0},{2,3},{3,2},{4,5},{5,4},{6,7},{7,6},{8,9},{9,8},{10,11... | collective-permute-start | bytes 1179656 | tf_op jit(solution)/shard_map/ppermute | solution.py:243
  227.8 14.7 %shard_map.124 = (bf16[64,3072]{1,0:T(8,128)(2,1)S(1)}, bf16[64,3072]{1,0:T(8,128)(2,1)S(1)}, bf16[64,3072]{1,0:T(8,128)(2,1)S(1)}, bf16[64,3072]{1,0:T(8,128)(2...) custom-call(s32[8]{0:T(128)S(1)} %iota_xor_fusion.refs_0_, ...), custom_call_target="tpu_custom_call" | custom-call | flops 1 | bytes 1 | tf_op jit(solution)/shard_map/pallas_call | solution.py:128
  251.3 14.1 %shard_map.128.refs_3_ = bf16[3072,3072]{1,0:T(8,128)(2,1)} custom-call(s32[8]{0:T(128)S(1)} %iota_xor_fusion.refs_0_, bf16[64,3072]{1,0:T(8,128)(2,1)S(1)} %copy-done.4, bf16[64,3072]{1,0:T(8,128)(2,1)S(1)} %get-tuple-element.41.refs_10_.refs_2_, bf16[128,3072]{1,0:T(8,128)(2,1)S(1)} %get-tuple-element.45.refs_3_, ...), custom_call_target="tpu_custom_call" | custom-call | flops 1 | bytes 1 | tf_op jit(solution)/shard_map/pallas_call | solution.py:128
  271.3 11.3 %shard_map.131 = (bf16[64,3072]{1,0:T(8,128)(2,1)S(1)}, bf16[64,3072]{1,0:T(8,128)(2,1)S(1)}, bf16[64,3072]{1,0:T(8,128)(2,1)S(1)}, bf16[64,3072]{1,0:T(8,128)(2,1)S(1)}) custom-call(s32[8]{0:T(128)S(1)} %iota_xor_fusion.refs_0_, bf16[128,3072]{1,0:T(8,128)(2,1)S(1)} %shard_map.127.refs_15_.refs_1_.refs_12_, ...), custom_call_target="tpu_custom_call" | custom-call | flops 1 | bytes 1 | tf_op jit(solution)/shard_map/pallas_call | solution.py:128
  288.5 11.6 %shard_map.133.refs_4_ = bf16[64,3072]{1,0:T(8,128)(2,1)S(1)} custom-call(s32[8]{0:T(128)S(1)} %iota_xor_fusion.refs_0_, bf16[64,3072]{1,0:T(8,128)(2,1)S(1)} %shard_map.110.refs_3_.refs_1_.refs_10_, bf16[3072,3072]{1,0:T(8,128)(2,1)} %refs_2_.11, s32[48,48]{1,0:T(8,128)S(1)} %copy-done.9, bf16[64,3072]{1,0:T(8,128)(2,1)S(1)} %shard_map.132.refs_4_.refs_1_.refs_9_), custom_call_target="tpu_custom_call" | custom-call | flops 1 | bytes 1 | tf_op jit(solution)/shard_map/pallas_call | solution.py:128
  305.0 11.4 %shard_map.134.refs_15_ = bf16[64,3072]{1,0:T(8,128)(2,1)S(1)} custom-call(s32[8]{0:T(128)S(1)} %iota_xor_fusion.refs_0_, bf16[64,3072]{1,0:T(8,128)(2,1)S(1)} %shard_map.132.refs_4_.refs_1_.refs_9_, bf16[3072,3072]{1,0:T(8,128)(2,1)} %refs_2_.11, s32[48,48]{1,0:T(8,128)S(1)} %copy-done.9, bf16[64,3072]{1,0:T(8,128)(2,1)S(1)} %shard_map.133.refs_4_), custom_call_target="tpu_custom_call" | custom-call | flops 1 | bytes 1 | tf_op jit(solution)/shard_map/pallas_call | solution.py:128
  318.5 14.7 %shard_map.135 = bf16[3072,3072]{1,0:T(8,128)(2,1)} custom-call(s32[8]{0:T(128)S(1)} %iota_xor_fusion.refs_0_, bf16[64,3072]{1,0:T(8,128)(2,1)} %refs_1_.3, bf16[64,3072]{1,0:T(8,128)(2,1)S(1)} %copy-done.23, bf16[64,3072]{1,0:T(8,128)(2,1)S(1)} %copy-done.21, bf16[64,3072]{1,0:T(8,128)(2,1)S(1)} %copy-done.27, bf16[64,3072]{1,0:T(8,128)(2,1)S(1)} %copy-done.19, ...), custom_call_target="tpu_custom_call" | custom-call | flops 1 | bytes 1 | tf_op jit(solution)/shard_map/pallas_call | solution.py:128
  (217 shorter events, 90.6 us)
Async XLA Ops:
  7.2 112.4 %all-gather.2.cloned.1.call-start = ((), (), s32[]{:S(2)}) async-start(), calls=%async_computation | async-start | bytes 3538944 | tf_op jit(solution)/shard_map/all_gather | solution.py:251
  12.5 27.3 %collective-permute-start.1 = (bf16[64,3072]{1,0:T(8,128)(2,1)}, bf16[64,3072]{1,0:T(8,128)(2,1)S(1)}, u32[]{:S(2)}, u32[]{:S(2)}) collective-permute-start(bf16[64,3072]{1,0:T(8,128)(2,1)} %refs_6_.5), channel_id=1, source_target_pairs={{0,1},{1,0},{2,3},{3,2},{4,5},{5,4},{6,7},{7,6},{8,9},{9,8},{10,11... | collective-permute-start | bytes 1179656 | tf_op jit(solution)/shard_map/ppermute | solution.py:243
  23.6 27.6 %collective-permute-start = (bf16[64,3072]{1,0:T(8,128)(2,1)S(1)}, bf16[64,3072]{1,0:T(8,128)(2,1)S(1)}, u32[]{:S(2)}, u32[]{:S(2)}) collective-permute-start(bf16[64,3072]{1,0:T(8,128)(2,1)S(1)} %shard_map.93.refs_4_.refs_1_), channel_id=1, source_target_pairs={{0,8},{24,16},{1,9},{25,17},{2,10},{26,18},{3,11},{27,19},{4,12},{... | collective-permute-start | bytes 1179656 | tf_op jit(solution)/shard_map/ppermute | solution.py:218
  26.9 25.9 %collective-permute-start.8 = (bf16[64,3072]{1,0:T(8,128)(2,1)S(1)}, bf16[64,3072]{1,0:T(8,128)(2,1)S(1)}, u32[]{:S(2)}, u32[]{:S(2)}) collective-permute-start(bf16[64,3072]{1,0:T(8,128)(2,1)S(1)} %collective-permute-done.7.refs_3_.refs_5_), channel_id=1, source_target_pairs={{0,1},{1,0},{2,3},{3,2},{4,5},{5,4},{6,7},{7,6},{8,9},{9,8},{10,11... | collective-permute-start | bytes 1179656 | tf_op jit(solution)/shard_map/ppermute | solution.py:243
  38.4 30.6 %collective-permute-start.4 = (bf16[64,3072]{1,0:T(8,128)(2,1)S(1)}, bf16[64,3072]{1,0:T(8,128)(2,1)S(1)}, u32[]{:S(2)}, u32[]{:S(2)}) collective-permute-start(bf16[64,3072]{1,0:T(8,128)(2,1)S(1)} %shard_map.94.refs_4_.refs_1_), channel_id=1, source_target_pairs={{0,8},{24,16},{1,9},{25,17},{2,10},{26,18},{3,11},{27,19},{4,12},{... | collective-permute-start | bytes 1179656 | tf_op jit(solution)/shard_map/ppermute | solution.py:218
  64.1 48.8 %collective-permute-start.14 = (bf16[128,3072]{1,0:T(8,128)(2,1)S(1)}, bf16[128,3072]{1,0:T(8,128)(2,1)S(1)}, u32[]{:S(2)}, u32[]{:S(2)}) collective-permute-start(bf16[128,3072]{1,0:T(8,128)(2,1)S(1)} %get-tuple-element.37.refs_3_.refs_1_), channel_id=1, source_target_pairs={{0,8},{24,16},{1,9},{25,17},{2,10},{26,18},{3,11},{27,19},{4,12},{... | collective-permute-start | bytes 2359304 | tf_op jit(solution)/shard_map/ppermute | solution.py:218
  106.4 33.1 %collective-permute-start.18 = (bf16[128,3072]{1,0:T(8,128)(2,1)S(1)}, bf16[128,3072]{1,0:T(8,128)(2,1)}, u32[]{:S(2)}, u32[]{:S(2)}) collective-permute-start(bf16[128,3072]{1,0:T(8,128)(2,1)S(1)} %get-tuple-element.42.refs_1_), channel_id=1, source_target_pairs={{0,8},{24,16},{1,9},{25,17},{2,10},{26,18},{3,11},{27,19},{4,12},{... | collective-permute-start | bytes 2359304 | tf_op jit(solution)/shard_map/ppermute | solution.py:218
  114.5 27.6 %collective-permute-start.17 = (bf16[128,3072]{1,0:T(8,128)(2,1)}, bf16[128,3072]{1,0:T(8,128)(2,1)}, u32[]{:S(2)}, u32[]{:S(2)}) collective-permute-start(bf16[128,3072]{1,0:T(8,128)(2,1)} %shard_map.104.refs_3_), channel_id=1, source_target_pairs={{8,16},{16,8},{9,17},{17,9},{10,18},{18,10},{11,19},{19,11},{12,20... | collective-permute-start | bytes 2359304 | tf_op jit(solution)/shard_map/ppermute | solution.py:218
  154.7 27.6 %collective-permute-start.23 = (bf16[128,3072]{1,0:T(8,128)(2,1)S(1)}, bf16[128,3072]{1,0:T(8,128)(2,1)S(1)}, u32[]{:S(2)}, u32[]{:S(2)}) collective-permute-start(bf16[128,3072]{1,0:T(8,128)(2,1)S(1)} %shard_map.112.refs_5_), channel_id=1, source_target_pairs={{16,24},{8,0},{17,25},{9,1},{18,26},{10,2},{19,27},{11,3},{20,28},... | collective-permute-start | bytes 2359304 | tf_op jit(solution)/shard_map/ppermute | solution.py:218
  156.0 30.1 %collective-permute-start.27 = (bf16[128,3072]{1,0:T(8,128)(2,1)S(1)}, bf16[128,3072]{1,0:T(8,128)(2,1)S(1)}, u32[]{:S(2)}, u32[]{:S(2)}) collective-permute-start(bf16[128,3072]{1,0:T(8,128)(2,1)S(1)} %get-tuple-element.47.refs_1_), channel_id=1, source_target_pairs={{0,8},{24,16},{1,9},{25,17},{2,10},{26,18},{3,11},{27,19},{4,12},{... | collective-permute-start | bytes 2359304 | tf_op jit(solution)/shard_map/ppermute | solution.py:218
  172.8 37.4 %collective-permute-start.30 = (bf16[128,3072]{1,0:T(8,128)(2,1)S(1)}, bf16[128,3072]{1,0:T(8,128)(2,1)S(1)}, u32[]{:S(2)}, u32[]{:S(2)}) collective-permute-start(bf16[128,3072]{1,0:T(8,128)(2,1)S(1)} %get-tuple-element.48.refs_1_), channel_id=1, source_target_pairs={{0,8},{24,16},{1,9},{25,17},{2,10},{26,18},{3,11},{27,19},{4,12},{... | collective-permute-start | bytes 2359304 | tf_op jit(solution)/shard_map/ppermute | solution.py:218
  186.9 36.6 %collective-permute-start.29 = (bf16[128,3072]{1,0:T(8,128)(2,1)S(1)}, bf16[128,3072]{1,0:T(8,128)(2,1)S(1)}, u32[]{:S(2)}, u32[]{:S(2)}) collective-permute-start(bf16[128,3072]{1,0:T(8,128)(2,1)S(1)} %shard_map.117.refs_3_), channel_id=1, source_target_pairs={{8,16},{16,8},{9,17},{17,9},{10,18},{18,10},{11,19},{19,11},{12,20... | collective-permute-start | bytes 2359304 | tf_op jit(solution)/shard_map/ppermute | solution.py:218
  188.4 37.4 %collective-permute-start.28 = (bf16[128,3072]{1,0:T(8,128)(2,1)S(1)}, bf16[128,3072]{1,0:T(8,128)(2,1)S(1)}, u32[]{:S(2)}, u32[]{:S(2)}) collective-permute-start(bf16[128,3072]{1,0:T(8,128)(2,1)S(1)} %shard_map.118.refs_6_), channel_id=1, source_target_pairs={{16,24},{8,0},{17,25},{9,1},{18,26},{10,2},{19,27},{11,3},{20,28},... | collective-permute-start | bytes 2359304 | tf_op jit(solution)/shard_map/ppermute | solution.py:218
  211.0 32.8 %collective-permute-start.42 = (bf16[128,3072]{1,0:T(8,128)(2,1)S(1)}, bf16[128,3072]{1,0:T(8,128)(2,1)S(1)}, u32[]{:S(2)}, u32[]{:S(2)}) collective-permute-start(bf16[128,3072]{1,0:T(8,128)(2,1)S(1)} %shard_map.121.refs_3_), channel_id=1, source_target_pairs={{8,16},{16,8},{9,17},{17,9},{10,18},{18,10},{11,19},{19,11},{12,20... | collective-permute-start | bytes 2359304 | tf_op jit(solution)/shard_map/ppermute | solution.py:218
  211.7 30.9 %collective-permute-start.39 = (bf16[64,3072]{1,0:T(8,128)(2,1)S(1)}, bf16[64,3072]{1,0:T(8,128)(2,1)S(1)}, u32[]{:S(2)}, u32[]{:S(2)}) collective-permute-start(bf16[64,3072]{1,0:T(8,128)(2,1)S(1)} %get-tuple-element.61.refs_1_), channel_id=1, source_target_pairs={{0,8},{24,16},{1,9},{25,17},{2,10},{26,18},{3,11},{27,19},{4,12},{... | collective-permute-start | bytes 1179656 | tf_op jit(solution)/shard_map/ppermute | solution.py:218
  215.8 28.9 %collective-permute-start.46 = (bf16[64,3072]{1,0:T(8,128)(2,1)S(1)}, bf16[64,3072]{1,0:T(8,128)(2,1)S(1)}, u32[]{:S(2)}, u32[]{:S(2)}) collective-permute-start(bf16[64,3072]{1,0:T(8,128)(2,1)S(1)} %get-tuple-element.66), channel_id=1, source_target_pairs={{0,1},{1,0},{2,3},{3,2},{4,5},{5,4},{6,7},{7,6},{8,9},{9,8},{10,11... | collective-permute-start | bytes 1179656 | tf_op jit(solution)/shard_map/ppermute | solution.py:243
  242.6 60.7 %collective-permute-start.32 = (bf16[64,3072]{1,0:T(8,128)(2,1)S(1)}, bf16[64,3072]{1,0:T(8,128)(2,1)}, u32[]{:S(2)}, u32[]{:S(2)}) collective-permute-start(bf16[64,3072]{1,0:T(8,128)(2,1)S(1)} %get-tuple-element.54), channel_id=1, source_target_pairs={{0,1},{1,0},{2,3},{3,2},{4,5},{5,4},{6,7},{7,6},{8,9},{9,8},{10,11... | collective-permute-start | bytes 1179656 | tf_op jit(solution)/shard_map/ppermute | solution.py:243
  243.8 25.9 %collective-permute-start.35 = (bf16[64,3072]{1,0:T(8,128)(2,1)S(1)}, bf16[64,3072]{1,0:T(8,128)(2,1)S(1)}, u32[]{:S(2)}, u32[]{:S(2)}) collective-permute-start(bf16[64,3072]{1,0:T(8,128)(2,1)S(1)} %get-tuple-element.58), channel_id=1, source_target_pairs={{0,1},{1,0},{2,3},{3,2},{4,5},{5,4},{6,7},{7,6},{8,9},{9,8},{10,11... | collective-permute-start | bytes 1179656 | tf_op jit(solution)/shard_map/ppermute | solution.py:243
  246.9 39.4 %collective-permute-start.37 = (bf16[64,3072]{1,0:T(8,128)(2,1)S(1)}, bf16[64,3072]{1,0:T(8,128)(2,1)S(1)}, u32[]{:S(2)}, u32[]{:S(2)}) collective-permute-start(bf16[64,3072]{1,0:T(8,128)(2,1)S(1)} %get-tuple-element.60), channel_id=1, source_target_pairs={{0,1},{1,0},{2,3},{3,2},{4,5},{5,4},{6,7},{7,6},{8,9},{9,8},{10,11... | collective-permute-start | bytes 1179656 | tf_op jit(solution)/shard_map/ppermute | solution.py:243
  265.5 67.8 %collective-permute-start.47 = (bf16[64,3072]{1,0:T(8,128)(2,1)}, bf16[64,3072]{1,0:T(8,128)(2,1)S(1)}, u32[]{:S(2)}, u32[]{:S(2)}) collective-permute-start(bf16[64,3072]{1,0:T(8,128)(2,1)} %add_convert_fusion.3), channel_id=1, source_target_pairs={{0,2},{1,3},{2,0},{3,1},{4,6},{5,7},{6,4},{7,5},{8,10},{9,11},{10,... | collective-permute-start | bytes 1179656 | tf_op jit(solution)/shard_map/ppermute | solution.py:243
  267.8 36.0 %collective-permute-start.34 = (bf16[64,3072]{1,0:T(8,128)(2,1)S(1)}, bf16[64,3072]{1,0:T(8,128)(2,1)S(1)}, u32[]{:S(2)}, u32[]{:S(2)}) collective-permute-start(bf16[64,3072]{1,0:T(8,128)(2,1)S(1)} %add_convert_fusion.7), channel_id=1, source_target_pairs={{0,2},{1,3},{2,0},{3,1},{4,6},{5,7},{6,4},{7,5},{8,10},{9,11},{10,... | collective-permute-start | bytes 1179656 | tf_op jit(solution)/shard_map/ppermute | solution.py:243
  303.3 30.0 %collective-permute-start.45 = (bf16[64,3072]{1,0:T(8,128)(2,1)S(1)}, bf16[64,3072]{1,0:T(8,128)(2,1)S(1)}, u32[]{:S(2)}, u32[]{:S(2)}) collective-permute-start(bf16[64,3072]{1,0:T(8,128)(2,1)S(1)} %shard_map.133.refs_4_), channel_id=1, source_target_pairs={{0,1},{1,0},{2,3},{3,2},{4,5},{5,4},{6,7},{7,6},{8,9},{9,8},{10,11... | collective-permute-start | bytes 1179656 | tf_op jit(solution)/shard_map/ppermute | solution.py:243
  303.8 29.5 %collective-permute-start.49 = (bf16[64,3072]{1,0:T(8,128)(2,1)S(1)}, bf16[64,3072]{1,0:T(8,128)(2,1)S(1)}, u32[]{:S(2)}, u32[]{:S(2)}) collective-permute-start(bf16[64,3072]{1,0:T(8,128)(2,1)S(1)} %add_convert_fusion.2), channel_id=1, source_target_pairs={{0,4},{1,5},{2,6},{3,7},{4,0},{5,1},{6,2},{7,3},{8,12},{9,13},{10,... | collective-permute-start | bytes 1179656 | tf_op jit(solution)/shard_map/ppermute | solution.py:243
  304.8 28.5 %collective-permute-start.51 = (bf16[64,3072]{1,0:T(8,128)(2,1)S(1)}, bf16[64,3072]{1,0:T(8,128)(2,1)S(1)}, u32[]{:S(2)}, u32[]{:S(2)}) collective-permute-start(bf16[64,3072]{1,0:T(8,128)(2,1)S(1)} %add_convert_fusion.1), channel_id=1, source_target_pairs={{0,6},{1,7},{2,4},{3,5},{4,2},{5,3},{6,0},{7,1},{8,14},{9,15},{10,... | collective-permute-start | bytes 1179656 | tf_op jit(solution)/shard_map/ppermute | solution.py:243
  (70 other events, 1547.4 us)
Sparse Core Ops, SparseCore 0:
  9.9 34.9 all-gather.1

commit v2 on v0

v2 whole, which is shorter than its diff:
```python
import functools
import math

import jax
import jax.numpy as jnp
from jax import lax
from jax.experimental import pallas as pl
from jax.experimental.pallas import tpu as pltpu
from jax.sharding import PartitionSpec as P

BLOCK = 64
HEAD_DIM = 128
TILE = 512
ROW_STEP = 16
SLOTS = 4
MATMUL_VMEM = 48 * 1024 * 1024
SUM_VMEM = 14 * 1024 * 1024
COST_STEP = 3500000
GELU_A = 0.7978845608
GELU_B = 0.044715


def lane_mask(mask_rows, width, first_block):
    blocks = mask_rows.shape[1]
    block = lax.broadcasted_iota(jnp.int32, (blocks, width), 0)
    column = lax.broadcasted_iota(jnp.int32, (blocks, width), 1)
    pick = (column // BLOCK + first_block == block).astype(jnp.float32)
    return jnp.dot(mask_rows.astype(jnp.float32), pick, preferred_element_type=jnp.float32)


def span(step, size):
    return pl.ds(pl.multiple_of(step * size, size), size)


def piece_copies(pieces, refs, target, sems):
    copies, at = [], 0
    for index, ((_, first, rows), ref) in enumerate(zip(pieces, refs)):
        copies.append(
            pltpu.make_async_copy(ref.at[pl.ds(first, rows), :], target.at[pl.ds(at, rows), :], sems.at[index])
        )
        at += rows
    return copies


def weight_kernel(pieces, transposed, tile, x_refs, tail, out_refs, scratch):
    w_ref, mask_hbm = tail
    x_all, w_in, w_kept, done, mask_ref, w_sems, x_sems, out_sems, mask_sem = scratch
    depth, width = w_kept.shape
    steps = w_ref.shape[0 if transposed else 1] // tile

    def fetch(step, slot):
        source = w_ref.at[span(step, tile), :] if transposed else w_ref.at[:, span(step, tile)]
        return pltpu.make_async_copy(source, w_in.at[slot], w_sems.at[slot])

    def leave(step, slot):
        copies, at = [], 0
        for index, out_ref in enumerate(out_refs):
            source = done.at[slot, pl.ds(at, out_ref.shape[0]), :]
            copies.append(
                pltpu.make_async_copy(source, out_ref.at[:, span(step, tile)], out_sems.at[slot, index])
            )
            at += out_ref.shape[0]
        return copies

    copies = piece_copies(pieces, x_refs, x_all, x_sems)
    copies.append(pltpu.make_async_copy(mask_hbm, mask_ref, mask_sem))
    fetch(0, 0).start()
    for copy in copies:
        copy.start()
    for step in range(1, min(SLOTS, steps)):
        fetch(step, step).start()
    for copy in copies:
        copy.wait()

    def body(step, carry):
        slot = lax.rem(step, SLOTS)
        fetch(step, slot).wait()
        if transposed:
            kept = lane_mask(mask_ref[span(step, tile // BLOCK), :], width, 0)
        else:
            kept = lane_mask(mask_ref[...], width, step * (tile // BLOCK))
        kept = kept.astype(jnp.bfloat16)
        for block in range(depth // BLOCK):
            rows = slice(block * BLOCK, (block + 1) * BLOCK)
            w_kept[rows, :] = w_in[slot, rows, :] * kept[block : block + 1, :]
        contract = ((1,), (1,)) if transposed else ((1,), (0,))
        product = lax.dot_general(
            x_all[...], w_kept[...], (contract, ((), ())), preferred_element_type=jnp.float32
        )

        @pl.when(step + SLOTS < steps)
        def _():
            fetch(step + SLOTS, slot).start()

        out_slot = lax.rem(step, 2)

        @pl.when(step >= 2)
        def _():
            for copy in leave(step - 2, out_slot):
                copy.wait()

        done[out_slot] = product.astype(done.dtype)
        for copy in leave(step, out_slot):
            copy.start()
        return carry

    lax.fori_loop(0, steps, body, 0)
    for step in range(max(0, steps - 2), steps):
        for copy in leave(step, step % 2):
            copy.wait()


def grad_kernel(x_pieces, g_pieces, scale, tile, refs, tail, out_refs, scratch):
    (mask_hbm,), (out_ref,) = tail, out_refs
    x_all, g_all, done, mask_ref, out_sems, sems, mask_sem = scratch
    count = len(x_pieces)
    copies = piece_copies(x_pieces, refs[:count], x_all, sems)
    copies += piece_copies(g_pieces, refs[count:], g_all, sems.at[pl.ds(count, len(g_pieces))])
    copies.append(pltpu.make_async_copy(mask_hbm, mask_ref, mask_sem))
    for copy in copies:
        copy.start()
    for copy in copies:
        copy.wait()
    depth, width = out_ref.shape
    blocks, steps, slots = tile // BLOCK, depth // tile, done.shape[0]

    def leave(step, slot):
        return pltpu.make_async_copy(done.at[slot], out_ref.at[span(step, tile), :], out_sems.at[slot])

    def body(step, carry):
        slot = lax.rem(step, slots)

        @pl.when(step >= slots)
        def _():
            leave(step - slots, slot).wait()

        kept = lane_mask(mask_ref[span(step, blocks), :], width, 0) * scale
        product = lax.dot_general(
            x_all[:, span(step, tile)], g_all[...], (((0,), (0,)), ((), ())), preferred_element_type=jnp.float32
        )
        for block in range(blocks):
            rows = slice(block * BLOCK, (block + 1) * BLOCK)
            done[slot, rows, :] = (product[rows, :] * kept[block : block + 1, :]).astype(done.dtype)
        leave(step, slot).start()
        return carry

    lax.fori_loop(0, steps, body, 0)
    for step in range(max(0, steps - slots), steps):
        leave(step, step % slots).wait()


def gelu_and_slope(value):
    square = value * value
    tanh = jnp.tanh(GELU_A * (value + GELU_B * (value * square)))
    half = 0.5 * (1.0 + tanh)
    slope = half + 0.5 * value * (1.0 - tanh * tanh) * (GELU_A * (1.0 + (3.0 * GELU_B) * square))
    return value * half, slope


def only_sum(total):
    return (total,)


def sum_kernel(finish, n_sum, splits, heads, refs, tail, out_refs, scratch):
    held, done, in_sems, out_sems = scratch
    width = refs[0].shape[1]
    fetches, first_row = [], 0
    for part, rows in enumerate(splits):
        span_from = pl.ds(first_row, rows)
        fetches.append(
            [
                pltpu.make_async_copy(ref.at[span_from, :], held.at[i, span_from, :], in_sems.at[part, i])
                for i, ref in enumerate(refs)
            ]
        )
        for fetch in fetches[-1]:
            fetch.start()
        first_row += rows
    leaves, first_row = [], 0
    for part, rows in enumerate(splits):
        for fetch in fetches[part]:
            fetch.wait()

        @pl.loop(0, rows // ROW_STEP)
        def _(step, first_row=first_row):
            at = pl.ds(pl.multiple_of(first_row + step * ROW_STEP, ROW_STEP), ROW_STEP)
            for first in range(0, width, TILE):
                columns = slice(first, first + TILE)
                values = [held[i, at, columns].astype(jnp.float32) for i in range(len(refs))]
                total = values[0]
                for value in values[1:n_sum]:
                    total = total + value
                for i, result in enumerate(finish(total, *values[n_sum:])):
                    if heads:
                        for lane in range(0, TILE, HEAD_DIM):
                            head = (first + lane) // HEAD_DIM
                            done[i, head, at, :] = result[:, lane : lane + HEAD_DIM].astype(done.dtype)
                    else:
                        done[i, at, columns] = result.astype(done.dtype)

        for i in range(done.shape[0]):
            source = done.at[i] if heads else done.at[i, pl.ds(first_row, rows), :]
            leaves.append(
                pltpu.make_async_copy(source, out_refs[i * len(splits) + part], out_sems.at[part, i])
            )
            leaves[-1].start()
        first_row += rows
    for leave in leaves:
        leave.wait()


def dispatch(kernel, counts, *refs):
    n_arrays, n_tail, n_pass, n_after, n_out = counts
    tail = refs[n_arrays : n_arrays + n_tail]
    outs = refs[n_arrays + n_tail + n_pass + n_after :]
    kernel(refs[:n_arrays], tail, outs[:n_out], outs[n_out + n_pass + 1 :])


class Order:
    def __init__(self):
        self.last = None

    def call(self, kernel, arrays, tail, outs, scratch, passing, vmem, weight=0.0):
        after = [] if self.last is None else [self.last]
        operands = list(arrays) + list(tail) + list(passing) + after
        token = jax.ShapeDtypeStruct((8, HEAD_DIM), jnp.float32)
        n_out, n_pass = len(outs), len(passing)
        first_pass = len(arrays) + len(tail)
        shapes = list(outs) + [jax.ShapeDtypeStruct(p.shape, p.dtype) for p in passing] + [token]
        *results, self.last = pl.pallas_call(
            functools.partial(dispatch, kernel, (len(arrays), len(tail), n_pass, len(after), n_out)),
            in_specs=[pl.BlockSpec(memory_space=pltpu.HBM)] * len(operands),
            out_specs=[pl.BlockSpec(memory_space=pltpu.HBM)] * len(shapes),
            scratch_shapes=scratch,
            out_shape=shapes,
            input_output_aliases={first_pass + i: n_out + i for i in range(n_pass)},
            compiler_params=pltpu.CompilerParams(vmem_limit_bytes=vmem),
            cost_estimate=pl.CostEstimate(flops=1, bytes_accessed=1 + int(weight * COST_STEP), transcendentals=0),
        )(*operands)
        return results

    def stacked(self, arrays):
        width = arrays[0].shape[1]
        pieces = [whole(array) for array in arrays]

        def kernel(refs, tail, out_refs, scratch):
            copies = piece_copies(pieces, refs, out_refs[0], scratch[0])
            for copy in copies:
                copy.start()
            for copy in copies:
                copy.wait()

        shape = (sum(array.shape[0] for array in arrays), width)
        return self.call(
            kernel,
            arrays,
            [],
            [jax.ShapeDtypeStruct(shape, jnp.bfloat16)],
            [pltpu.SemaphoreType.DMA((len(arrays),))],
            (),
            SUM_VMEM,
        )[0]

    def tied(self, arrays):
        return self.call(lambda refs, tail, out_refs, scratch: None, [], [], [], [], arrays, SUM_VMEM)

    def times_weight(self, pieces, weight, mask, splits, transposed, passing=(), tile=TILE):
        depth, width = weight.shape
        x_width, out_width = (width, depth) if transposed else (depth, width)
        rows = sum(piece[2] for piece in pieces)
        w_block = (tile, width) if transposed else (depth, tile)
        return self.call(
            functools.partial(weight_kernel, pieces, transposed, tile),
            [piece[0] for piece in pieces],
            [weight, mask],
            [jax.ShapeDtypeStruct((split, out_width), jnp.bfloat16) for split in splits],
            [
                pltpu.VMEM((rows, x_width), jnp.bfloat16),
                pltpu.VMEM((SLOTS,) + w_block, jnp.bfloat16),
                pltpu.VMEM(w_block, jnp.bfloat16),
                pltpu.VMEM((2, rows, tile), jnp.bfloat16),
                pltpu.VMEM(mask.shape, mask.dtype),
                pltpu.SemaphoreType.DMA((SLOTS,)),
                pltpu.SemaphoreType.DMA((len(pieces),)),
                pltpu.SemaphoreType.DMA((2, len(splits))),
                pltpu.SemaphoreType.DMA,
            ],
            passing,
            MATMUL_VMEM,
            7.0 + 0.02 * max(0, rows - 128),
        )

    def weight_grad(self, x_pieces, g_pieces, mask, scale, passing=(), tile=TILE):
        pieces = list(x_pieces) + list(g_pieces)
        depth, width = x_pieces[0][0].shape[1], g_pieces[0][0].shape[1]
        return self.call(
            functools.partial(grad_kernel, x_pieces, g_pieces, scale, tile),
            [piece[0] for piece in pieces],
            [mask],
            [jax.ShapeDtypeStruct((depth, width), jnp.bfloat16)],
            [
                pltpu.VMEM((sum(piece[2] for piece in x_pieces), depth), jnp.bfloat16),
                pltpu.VMEM((sum(piece[2] for piece in g_pieces), width), jnp.bfloat16),
                pltpu.VMEM((2, tile, width), jnp.bfloat16),
                pltpu.VMEM(mask.shape, mask.dtype),
                pltpu.SemaphoreType.DMA((2,)),
                pltpu.SemaphoreType.DMA((len(pieces),)),
                pltpu.SemaphoreType.DMA,
            ],
            passing,
            MATMUL_VMEM,
            15.0,
        )

    def summed(self, finish, arrays, others=(), n_out=1, splits=None, heads=False, passing=()):
        rows, width = arrays[0].shape
        splits = splits or [rows]
        operands = list(arrays) + list(others)
        shapes = [(width // HEAD_DIM, rows, HEAD_DIM)] if heads else [(split, width) for split in splits]
        whole_shape = shapes[0] if heads else (rows, width)
        outs = [jax.ShapeDtypeStruct(shape, jnp.bfloat16) for shape in shapes] * n_out
        return self.call(
            functools.partial(sum_kernel, finish, len(arrays), splits, heads),
            operands,
            [],
            outs,
            [
                pltpu.VMEM((len(operands), rows, width), jnp.bfloat16),
                pltpu.VMEM((n_out,) + whole_shape, jnp.bfloat16),
                pltpu.SemaphoreType.DMA((len(splits), len(operands))),
                pltpu.SemaphoreType.DMA((len(splits), n_out)),
            ],
            passing,
            SUM_VMEM,
        )


class Chain:
    def __init__(self, order, n_row):
        self.order, self.n_row, self.got = order, n_row, []

    def send(self, value):
        hop = len(self.got)
        pairs = [(hop, hop + 1), (self.n_row - 1 - hop, self.n_row - 2 - hop)]
        self.got.append(lax.ppermute(value, "row", pairs))

    def start(self, part):
        self.part = part
        self.send(part)

    def advance(self):
        self.send(self.order.summed(only_sum, [self.part, self.got[-1]])[0])

    def total(self, finish, others, n_out):
        return self.order.summed(finish, [self.part] + self.got, others, n_out)


def whole(array):
    return (array, 0, array.shape[0])


def halving(n_col):
    places = [0]
    bit = n_col // 2
    while bit:
        places = places + [place + bit for place in places]
        bit //= 2
    return places


def body(tokens, up_weight, up_mask, down_weight, down_mask, grad_out):
    n_row, n_col = lax.axis_size("row"), lax.axis_size("col")
    share = tokens.shape[0]
    grad_scale = 1.0 / math.sqrt(share * n_col)
    chips = n_col // 2
    order = Order()

    def swap(value, offset):
        return lax.ppermute(value, "col", [(i, i ^ offset) for i in range(n_col)])

    tok, cot = [whole(tokens)] + [None] * (n_col - 1), [whole(grad_out)] + [None] * (n_col - 1)
    for offset in range(1, min(6, n_col)):
        tok[offset] = whole(swap(tokens, offset))

    def hold_stacked(offset, value):
        tok[offset], cot[offset] = (value, 0, share), (value, share, share)

    offsets = [[2 * chip, 2 * chip + 1] for chip in range(chips)]
    queue = [("a", c) for c in range(chips)] + [("b", c) for c in range(1, chips)] + [("b", 0)]
    chains = {key: Chain(order, n_row) for key in queue}
    parts, hidden, slope, grad_pre = {}, {}, {}, {}
    results, tok_sums = {}, {}

    def shard_of(held, offset):
        return (held[offset // 2], (offset % 2) * share, share)

    def finish(key):
        kind, chunk = key
        if kind == "a":
            hidden[chunk], slope[chunk] = chains[key].total(gelu_and_slope, [], 2)
        else:
            (grad_pre[chunk],) = chains[key].total(lambda total, rise: (total * rise,), [slope[chunk]], 1)

    def partial(kind, chunks):
        source, weight, mask = (tok, up_weight, up_mask) if kind == "a" else (cot, down_weight, down_mask)

        def run(passing=()):
            pieces = [source[offset] for chunk in chunks for offset in offsets[chunk]]
            outs = order.times_weight(pieces, weight, mask, [2 * share] * len(chunks), kind == "b", passing)
            for chunk, out in zip(chunks, outs):
                parts[kind, chunk] = out
            return outs[len(chunks) :]

        return run

    def work_out(passing=()):
        pieces = [shard_of(hidden, offset) for offset in halving(n_col)]
        half = share * n_col // 2
        results["keep"], results["give"], *passed = order.times_weight(
            pieces, down_weight, down_mask, [half, half], False, passing
        )
        results["bit"] = 1
        return passed

    def give_out():
        (give,) = order.tied([results["give"]])
        results["got"] = swap(give, results["bit"])

    def halve_out(passing=()):
        rows = results["keep"].shape[0]
        arrays = [results["keep"], results["got"]]
        if rows == share:
            results["out"], *passed = order.summed(only_sum, arrays, heads=True, passing=passing)
            return passed
        results["keep"], results["give"], *passed = order.summed(
            only_sum, arrays, splits=[rows // 2, rows // 2], passing=passing
        )
        results["bit"] *= 2
        return passed

    def work_down(passing=()):
        results["down"], *passed = order.weight_grad(
            [whole(hidden[c]) for c in range(chips)],
            [cot[offset] for chunk in offsets for offset in chunk],
            down_mask,
            grad_scale,
            passing,
        )
        return passed

    pending = []

    def work_tok(chunks):
        def run(passing=()):
            kept = [offset for chunk in chunks for offset in offsets[chunk] if offset % 2 == 0]
            given = [offset for chunk in chunks for offset in offsets[chunk] if offset % 2]
            pieces = [shard_of(grad_pre, offset) for offset in kept + given]
            splits = [share * len(group) for group in (kept, given) if group]
            outs = order.times_weight(pieces, up_weight, up_mask, splits, True, passing)
            if chunks == [0]:
                tok_sums[0], tok_sums[1] = outs[0], swap(outs[1], 1)
            else:
                pending.append((kept, outs[0], swap(outs[1], 1)))
            return outs[len(splits) :]

        return run

    def pair_sums():
        while pending:
            kept, keep, got = pending.pop(0)
            sums = order.summed(only_sum, [keep, got], splits=[share] * len(kept))
            for offset, value in zip(kept, sums):
                tok_sums[offset] = swap(value, offset)

    last_slot = len(queue) + n_row - 3
    place_of = {key: i for i, key in enumerate(queue)}

    def ready(key):
        return place_of[key] + n_row - 2

    work = {slot: [] for slot in range(last_slot + 1)}
    work[1].append(partial("a", list(range(3, chips))))
    work[2].append(partial("b", list(range(1, chips)) + [0]))
    last_a = ready(("a", chips - 1))
    work[last_a].append(work_out)
    work[last_a + 1].append(work_down)
    held = []
    for chunk in range(1, chips):
        held.append(chunk)
        if ready(("b", chunk)) > last_a + 1:
            work[ready(("b", chunk))].append(work_tok(held))
            held = []

    started = 1

    def start_next(step):
        nonlocal started
        key = queue[started] if started < len(queue) else None
        passing = (parts[key],) if key in parts else ()
        passed = step(passing) if step else order.tied(passing) if passing else ()
        if key is not None:
            parts[key] = passed[0] if passing else parts[key]
            chains[key].start(parts[key])
            started += 1

    partial("a", [0])()
    chains[queue[0]].start(parts[queue[0]])
    start_next(partial("a", list(range(1, min(3, chips)))))
    both = order.stacked([tokens, grad_out])
    late_cot = order.stacked([grad_out])
    near = [(offset, swap(late_cot, offset)) for offset in range(2, min(6, n_col), 2)]
    for slot in range(last_slot + 1):
        for hop in range(n_row - 1):
            at = slot - hop
            if 0 <= at < len(queue):
                if hop < n_row - 2:
                    chains[queue[at]].advance()
                else:
                    finish(queue[at])
        if slot == 0:
            values = order.tied([value for _, value in near])
            for (offset, _), value in zip(near, values):
                cot[offset], cot[offset + 1] = whole(value), whole(swap(value, 1))
            (both,) = order.tied([both])
            far = [(offset, swap(both, offset)) for offset in range(6, n_col, 2)]
        if slot == 1:
            values = order.tied([value for _, value in far] + [late_cot])
            for (offset, _), value in zip(far, values):
                hold_stacked(offset, value)
                hold_stacked(offset + 1, swap(value, 1))
            cot[1] = whole(swap(values[-1], 1))
        pair_sums()
        steps = list(work[slot])
        if slot > last_a and "out" not in results:
            give_out()
            steps.append(halve_out)
        for step in steps[:-1]:
            step()
        start_next(steps[-1] if steps else None)

    work_tok([0])()
    while "out" not in results:
        give_out()
        halve_out()
    (up,) = order.weight_grad(
        [tok[offset] for chunk in offsets for offset in chunk],
        [whole(grad_pre[c]) for c in range(chips)],
        up_mask,
        grad_scale,
    )
    (grad_tokens,) = order.summed(only_sum, [tok_sums[offset] for offset in sorted(tok_sums)])
    return (results["out"], grad_tokens, up, results["down"])


def solution(mesh):
    return jax.shard_map(
        body,
        mesh=mesh,
        in_specs=(
            P("col", "row"),
            P("row", "col"),
            P("row", "col"),
            P("col", "row"),
            P("col", "row"),
            P("col", "row"),
        ),
        out_specs=(P("row", "col", None), P("col", "row"), P("row", "col"), P("col", "row")),
        check_vma=False,
    )
```

time: 616 us -> 289 us (0.47)
  local copies, waits for them, and re-layouts: 324 us -> 16.4 us
  Pallas kernels: 0 us -> 146 us
  matrix products: 118 us -> 0 us
  waiting for transfers between devices: 126 us -> 42.4 us
  starting transfers between devices: 0.72 us -> 80.9 us
  other arithmetic: 27 us -> 0 us
  between operations: 14.2 us -> 1.96 us
    mul x8 -> x0, local copies, waits for them, and re-layouts: 286 us -> none  [expand(): tiles = tiles * mask.astype(weight.dtype)[:, None, :, None]]
    pallas_call x0 -> x51, Pallas kernels: none -> 146 us  [call(): pl.pallas_call(functools.partial(dispatch, kernel, (len(arrays), len(tail...]
    dot_general x6 -> x0, matrix products: 118 us -> none  [the longest x2 49.8 us: over_tokens(): lax.dot_general(left, right, (((0,), (0,)), ((), ())), preferred_element_...]
    ppermute x0 -> x45, starting transfers between devices: none -> 80.9 us  [the longest x24 52.1 us: send(): self.got.append(lax.ppermute(value, 'row', pairs))]
    all_gather x4 -> x0, waiting for transfers between devices: 63.1 us -> none  [the longest x1 63 us: body(): hidden_all = lax.all_gather(hidden, 'row', axis=0, tiled=True)]
    unnamed x10 -> x0, waiting for transfers between devices: 62.5 us -> none
    ppermute x0 -> x45, waiting for transfers between devices: none -> 42.4 us  [the longest x24 22.9 us: send(): self.got.append(lax.ppermute(value, 'row', pairs))]
    mul x1 -> x0, other arithmetic: 23.7 us -> none  [expand(): tiles = tiles * mask.astype(weight.dtype)[:, None, :, None]]
  transfers between devices with their start and end apart: 8 -> 45, of which waited for: 2 -> 13; matrix products, arithmetic and copies ran while one was open for 76% -> 0% of each run, Pallas kernels for 0% -> 49%
where the time goes in v2:
time: 289 us; the launch traced here: 288 us
  Pallas kernels  146 us (51%)
  starting transfers between devices  80.9 us (28%)
  waiting for transfers between devices  42.4 us (15%)
  local copies, waits for them, and re-layouts  16.4 us (6%)
    pallas_call x51, Pallas kernels, call(): pl.pallas_call(functools.partial(dispatch, kernel, (len(arrays), len(tail...  146 us
    ppermute x24, starting transfers between devices, send(): self.got.append(lax.ppermute(value, 'row', pairs))  52.1 us
    ppermute x21, starting transfers between devices, swap(): return lax.ppermute(value, 'col', [(i, i ^ offset) for i in range(n_col)])  28.8 us
    ppermute x24, waiting for transfers between devices, send(): self.got.append(lax.ppermute(value, 'row', pairs))  22.9 us
    ppermute x21, waiting for transfers between devices, swap(): return lax.ppermute(value, 'col', [(i, i ^ offset) for i in range(n_col)])  19.5 us
    unnamed x94, local copies, waits for them, and re-layouts  16.4 us
  transfers between devices with their start and end apart: 45, of which 13 were waited for; matrix products, arithmetic and copies ran while one was open for 0% of the time, Pallas kernels for 49%

profile of v2, /device:TPU:1, one launch (start us, length us, event | category | flops | bytes accessed | tf_op | source)
XLA Modules:
  0.0 287.7 jit_solution(13267368821380107594)
XLA Ops:
  7.3 7.8 %shard_map.93 = (bf16[128,3072]{1,0:T(8,128)(2,1)S(1)}, f32[8,128]{1,0:T(8,128)S(1)}) custom-call(bf16[64,3072]{1,0:T(8,128)(2,1)S(1)} %copy-done.7, bf16[64,3072]{1,0:T(8,128)(2,1)S(1)} %collective-permute-done.refs_1_, bf16[3072,3072]{1,0:T(8,128)(2,1)} %refs_2_.7, s32[48,48]{1,0:T(8,128)S(1)} %copy-done.32), custom_call_target="tpu_custom_call" | custom-call | flops 1 | bytes 24500000 | tf_op jit(solution)/shard_map/pallas_call | solution.py:230
  15.1 3.5 %collective-permute-start.1 = (bf16[128,3072]{1,0:T(8,128)(2,1)S(1)}, bf16[128,3072]{1,0:T(8,128)(2,1)S(1)}, u32[]{:S(2)}, u32[]{:S(2)}) collective-permute-start(bf16[128,3072]{1,0:T(8,128)(2,1)S(1)} %get-tuple-element.123.refs_0_), channel_id=1, source_target_pairs={{0,8},{24,16},{1,9},{25,17},{2,10},{26,18},{3,11},{27,19},{4,12},{... | collective-permute-start | bytes 2359304 | tf_op jit(solution)/shard_map/ppermute | solution.py:345
  23.1 9.2 %shard_map.94 = (bf16[128,3072]{1,0:T(8,128)(2,1)S(1)}, bf16[128,3072]{1,0:T(8,128)(2,1)S(1)}, f32[8,128]{1,0:T(8,128)S(1)}) custom-call(bf16[64,3072]{1,0:T(8,128)(2,1)S(1)} %collective-permute-done.2.refs_0_.refs_2_, bf16[64,3072]{1,0:T(8,128)(2,1)S(1)} %collective-permute-done.3.refs_1_.refs_3_, ...), custom_call_target="tpu_custom_call" | custom-call | flops 1 | bytes 33460000 | tf_op jit(solution)/shard_map/pallas_call | solution.py:230
  40.9 3.3 %collective-permute-done.9.refs_1_ = bf16[64,3072]{1,0:T(8,128)(2,1)S(1)} collective-permute-done((bf16[64,3072]{1,0:T(8,128)(2,1)S(1)}, bf16[64,3072]{1,0:T(8,128)(2,1)S(1)}, u32[]{:S(2)}, u32[]{:S(2)}) %collective-permute-start.9) | collective-permute-done | bytes 393248 | tf_op jit(solution)/shard_map/ppermute | solution.py:379
  49.7 5.8 %collective-permute-done.7.refs_1_ = bf16[128,3072]{1,0:T(8,128)(2,1)S(1)} collective-permute-done((bf16[128,3072]{1,0:T(8,128)(2,1)S(1)}, bf16[128,3072]{1,0:T(8,128)(2,1)S(1)}, u32[]{:S(2)}, u32[]{:S(2)}) %collective-permute-start.7) | collective-permute-done | bytes 786464 | tf_op jit(solution)/shard_map/ppermute | solution.py:345
  56.4 6.9 %collective-permute-done.13.refs_0_ = bf16[128,3072]{1,0:T(8,128)(2,1)S(1)} collective-permute-done((bf16[128,3072]{1,0:T(8,128)(2,1)S(1)}, bf16[128,3072]{1,0:T(8,128)(2,1)S(1)}, u32[]{:S(2)}, u32[]{:S(2)}) %collective-permute-start.13) | collective-permute-done | bytes 786464 | tf_op jit(solution)/shard_map/ppermute | solution.py:379
  68.0 4.4 %collective-permute-done.12.refs_1_ = bf16[128,3072]{1,0:T(8,128)(2,1)S(1)} collective-permute-done((bf16[128,3072]{1,0:T(8,128)(2,1)S(1)}, bf16[128,3072]{1,0:T(8,128)(2,1)S(1)}, u32[]{:S(2)}, u32[]{:S(2)}) %collective-permute-start.12) | collective-permute-done | bytes 786464 | tf_op jit(solution)/shard_map/ppermute | solution.py:345
  74.3 7.8 %shard_map.104 = (bf16[128,3072]{1,0:T(8,128)(2,1)S(1)}, f32[8,128]{1,0:T(8,128)S(1)}) custom-call(bf16[128,3072]{1,0:T(8,128)(2,1)S(1)} %get-tuple-element.143.refs_0_.refs_4_.refs_10_.refs_6_, bf16[128,3072]{1,0:T(8,128)(2,1)S(1)} %collective-permute-done.14.refs_1_.refs_5_.refs_11_.refs_7_, bf16[3072,3072]{1,0:T(8,128)(2,1)} %refs_2_.7, ...), custom_call_target="tpu_custom_call" | custom-call | flops 1 | bytes 24500000 | tf_op jit(solution)/shard_map/pallas_call | solution.py:230
  83.4 6.8 %collective-permute-start.16 = (bf16[128,3072]{1,0:T(8,128)(2,1)S(1)}, bf16[128,3072]{1,0:T(8,128)(2,1)S(1)}, u32[]{:S(2)}, u32[]{:S(2)}) collective-permute-start(bf16[128,3072]{1,0:T(8,128)(2,1)S(1)} %get-tuple-element.150.refs_0_), channel_id=1, source_target_pairs={{0,8},{24,16},{1,9},{25,17},{2,10},{26,18},{3,11},{27,19},{4,12},{... | collective-permute-start | bytes 2359304 | tf_op jit(solution)/shard_map/ppermute | solution.py:345
  98.1 14.8 %shard_map.108 = (bf16[128,3072]{1,0:T(8,128)(2,1)S(1)}, bf16[128,3072]{1,0:T(8,128)(2,1)S(1)}, bf16[128,3072]{1,0:T(8,128)(2,1)S(1)}, bf16[128,3072]{1,0:T(8,128)(2,1)S(1)}, f32[8,128]{1,0:T(8,128)S(1)}) custom-call(bf16[64,3072]{1,0:T(8,128)(2,1)S(1)} %get-tuple-element.151.refs_0_.refs_6_, bf16[64,3072]{1,0:T(8,128)(2,1)S(1)} %collective-permute-done.17.refs_1_.refs_7_, ...), custom_call_target="tpu_custom_call" | custom-call | flops 1 | bytes 51380000 | tf_op jit(solution)/shard_map/pallas_call | solution.py:230
  112.9 4.1 %collective-permute-start.22 = (bf16[128,3072]{1,0:T(8,128)(2,1)S(1)}, bf16[128,3072]{1,0:T(8,128)(2,1)S(1)}, u32[]{:S(2)}, u32[]{:S(2)}) collective-permute-start(bf16[128,3072]{1,0:T(8,128)(2,1)S(1)} %get-tuple-element.159.refs_0_), channel_id=1, source_target_pairs={{0,8},{24,16},{1,9},{25,17},{2,10},{26,18},{3,11},{27,19},{4,12},{... | collective-permute-start | bytes 2359304 | tf_op jit(solution)/shard_map/ppermute | solution.py:345
  124.7 4.1 %collective-permute-start.26 = (bf16[128,3072]{1,0:T(8,128)(2,1)S(1)}, bf16[128,3072]{1,0:T(8,128)(2,1)S(1)}, u32[]{:S(2)}, u32[]{:S(2)}) collective-permute-start(bf16[128,3072]{1,0:T(8,128)(2,1)S(1)} %get-tuple-element.171.refs_0_), channel_id=1, source_target_pairs={{0,8},{24,16},{1,9},{25,17},{2,10},{26,18},{3,11},{27,19},{4,12},{... | collective-permute-start | bytes 2359304 | tf_op jit(solution)/shard_map/ppermute | solution.py:345
  128.7 3.7 %collective-permute-done.22.refs_1_ = bf16[128,3072]{1,0:T(8,128)(2,1)S(1)} collective-permute-done((bf16[128,3072]{1,0:T(8,128)(2,1)S(1)}, bf16[128,3072]{1,0:T(8,128)(2,1)S(1)}, u32[]{:S(2)}, u32[]{:S(2)}) %collective-permute-start.22) | collective-permute-done | bytes 786464 | tf_op jit(solution)/shard_map/ppermute | solution.py:345
  140.9 4.1 %collective-permute-start.29 = (bf16[128,3072]{1,0:T(8,128)(2,1)S(1)}, bf16[128,3072]{1,0:T(8,128)(2,1)S(1)}, u32[]{:S(2)}, u32[]{:S(2)}) collective-permute-start(bf16[128,3072]{1,0:T(8,128)(2,1)S(1)} %get-tuple-element.185.refs_0_), channel_id=1, source_target_pairs={{0,8},{24,16},{1,9},{25,17},{2,10},{26,18},{3,11},{27,19},{4,12},{... | collective-permute-start | bytes 2359304 | tf_op jit(solution)/shard_map/ppermute | solution.py:345
  144.9 4.3 %collective-permute-done.26.refs_1_ = bf16[128,3072]{1,0:T(8,128)(2,1)S(1)} collective-permute-done((bf16[128,3072]{1,0:T(8,128)(2,1)S(1)}, bf16[128,3072]{1,0:T(8,128)(2,1)S(1)}, u32[]{:S(2)}, u32[]{:S(2)}) %collective-permute-start.26) | collective-permute-done | bytes 786464 | tf_op jit(solution)/shard_map/ppermute | solution.py:345
  156.7 14.9 %shard_map.120 = (bf16[256,3072]{1,0:T(8,128)(2,1)S(1)}, bf16[256,3072]{1,0:T(8,128)(2,1)}, bf16[128,3072]{1,0:T(8,128)(2,1)S(1)}, f32[8,128]{1,0:T(8,128)S(1)}) custom-call(bf16[128,3072]{1,0:T(8,128)(2,1)S(1)} %get-tuple-element.148.refs_0_.refs_4_, ...), custom_call_target="tpu_custom_call", output_to_operand_aliasing={{2}: (10, {})} | custom-call | flops 1 | bytes 51380000 | tf_op jit(solution)/shard_map/pallas_call | solution.py:230
  178.4 4.5 %collective-permute-start.30 = (bf16[256,3072]{1,0:T(8,128)(2,1)}, bf16[256,3072]{1,0:T(8,128)(2,1)S(1)}, u32[]{:S(2)}, u32[]{:S(2)}) collective-permute-start(bf16[256,3072]{1,0:T(8,128)(2,1)} %get-tuple-element.190), channel_id=1, source_target_pairs={{0,1},{1,0},{2,3},{3,2},{4,5},{5,4},{6,7},{7,6},{8,9},{9,8},{10,11... | collective-permute-start | bytes 4718600 | tf_op jit(solution)/shard_map/ppermute | solution.py:379
  182.9 6.6 %collective-permute-start.33 = (bf16[128,3072]{1,0:T(8,128)(2,1)S(1)}, bf16[128,3072]{1,0:T(8,128)(2,1)S(1)}, u32[]{:S(2)}, u32[]{:S(2)}) collective-permute-start(bf16[128,3072]{1,0:T(8,128)(2,1)S(1)} %get-tuple-element.198.refs_0_), channel_id=1, source_target_pairs={{0,8},{24,16},{1,9},{25,17},{2,10},{26,18},{3,11},{27,19},{4,12},{... | collective-permute-start | bytes 2359304 | tf_op jit(solution)/shard_map/ppermute | solution.py:345
  191.6 15.3 %shard_map.125 = (bf16[3072,3072]{1,0:T(8,128)(2,1)}, f32[8,128]{1,0:T(8,128)S(1)}) custom-call(bf16[128,3072]{1,0:T(8,128)(2,1)S(1)} %get-tuple-element.148.refs_0_.refs_4_, bf16[128,3072]{1,0:T(8,128)(2,1)S(1)} %get-tuple-element.168.refs_2_.refs_6_.refs_1_, bf16[128,3072]{1,0:T(8,128)(2,1)S(1)} %get-tuple-element.167.refs_1_.refs_5_.refs_2_, ...), custom_call_target="tpu_custom_call" | custom-call | flops 1 | bytes 52500000 | tf_op jit(solution)/shard_map/pallas_call | solution.py:230
  217.9 9.2 %shard_map.131 = (bf16[128,3072]{1,0:T(8,128)(2,1)S(1)}, bf16[128,3072]{1,0:T(8,128)(2,1)S(1)}, f32[8,128]{1,0:T(8,128)S(1)}) custom-call(bf16[128,3072]{1,0:T(8,128)(2,1)S(1)} %get-tuple-element.204.refs_0_.refs_2_.refs_9_, bf16[128,3072]{1,0:T(8,128)(2,1)S(1)} %get-tuple-element.205.refs_1_.refs_3_.refs_10_, ...), custom_call_target="tpu_custom_call" | custom-call | flops 1 | bytes 33460000 | tf_op jit(solution)/shard_map/pallas_call | solution.py:230
  228.6 3.8 %collective-permute-done.34.refs_1_ = bf16[128,3072]{1,0:T(8,128)(2,1)S(1)} collective-permute-done((bf16[128,3072]{1,0:T(8,128)(2,1)S(1)}, bf16[128,3072]{1,0:T(8,128)(2,1)S(1)}, u32[]{:S(2)}, u32[]{:S(2)}) %collective-permute-start.34) | collective-permute-done | bytes 786464 | tf_op jit(solution)/shard_map/ppermute | solution.py:379
  239.6 10.2 %shard_map.137 = (bf16[64,3072]{1,0:T(8,128)(2,1)S(1)}, bf16[64,3072]{1,0:T(8,128)(2,1)S(1)}, f32[8,128]{1,0:T(8,128)S(1)}) custom-call(bf16[128,3072]{1,0:T(8,128)(2,1)S(1)} %get-tuple-element.220.refs_0_.refs_1_.refs_11_, bf16[128,3072]{1,0:T(8,128)(2,1)S(1)} %get-tuple-element.220.refs_0_.refs_1_.refs_11_, bf16[3072,3072]{1,0:T(8,128)(2,1)} %refs_2_.7, ...), custom_call_target="tpu_custom_call" | custom-call | flops 1 | bytes 24500000 | tf_op jit(solution)/shard_map/pallas_call | solution.py:230
  257.8 10.0 %shard_map.141 = (bf16[64,3072]{1,0:T(8,128)(2,1)S(1)}, bf16[64,3072]{1,0:T(8,128)(2,1)S(1)}, f32[8,128]{1,0:T(8,128)S(1)}) custom-call(bf16[128,3072]{1,0:T(8,128)(2,1)S(1)} %get-tuple-element.227.refs_0_.refs_1_.refs_8_, bf16[128,3072]{1,0:T(8,128)(2,1)S(1)} %get-tuple-element.227.refs_0_.refs_1_.refs_8_, bf16[3072,3072]{1,0:T(8,128)(2,1)} %refs_2_.7, ...), custom_call_target="tpu_custom_call" | custom-call | flops 1 | bytes 24500000 | tf_op jit(solution)/shard_map/pallas_call | solution.py:230
  269.6 15.8 %shard_map.142 = (bf16[3072,3072]{1,0:T(8,128)(2,1)}, f32[8,128]{1,0:T(8,128)S(1)}) custom-call(bf16[64,3072]{1,0:T(8,128)(2,1)S(1)} %copy-done.8, bf16[64,3072]{1,0:T(8,128)(2,1)S(1)} %copy-done.31, bf16[64,3072]{1,0:T(8,128)(2,1)S(1)} %copy-done.22, bf16[64,3072]{1,0:T(8,128)(2,1)S(1)} %copy-done.20, bf16[64,3072]{1,0:T(8,128)(2,1)S(1)} %copy-done.18, ...), custom_call_target="tpu_custom_call" | custom-call | flops 1 | bytes 52500000 | tf_op jit(solution)/shard_map/pallas_call | solution.py:230
  (211 shorter events, 104.8 us)
Async XLA Ops:
  15.1 24.6 %collective-permute-start.1 = (bf16[128,3072]{1,0:T(8,128)(2,1)S(1)}, bf16[128,3072]{1,0:T(8,128)(2,1)S(1)}, u32[]{:S(2)}, u32[]{:S(2)}) collective-permute-start(bf16[128,3072]{1,0:T(8,128)(2,1)S(1)} %get-tuple-element.123.refs_0_), channel_id=1, source_target_pairs={{0,8},{24,16},{1,9},{25,17},{2,10},{26,18},{3,11},{27,19},{4,12},{... | collective-permute-start | bytes 2359304 | tf_op jit(solution)/shard_map/ppermute | solution.py:345
  46.4 26.0 %collective-permute-start.12 = (bf16[128,3072]{1,0:T(8,128)(2,1)S(1)}, bf16[128,3072]{1,0:T(8,128)(2,1)S(1)}, u32[]{:S(2)}, u32[]{:S(2)}) collective-permute-start(bf16[128,3072]{1,0:T(8,128)(2,1)S(1)} %get-tuple-element.140.refs_0_), channel_id=1, source_target_pairs={{0,8},{24,16},{1,9},{25,17},{2,10},{26,18},{3,11},{27,19},{4,12},{... | collective-permute-start | bytes 2359304 | tf_op jit(solution)/shard_map/ppermute | solution.py:345
  66.6 24.9 %collective-permute-start.10 = (bf16[128,3072]{1,0:T(8,128)(2,1)S(1)}, bf16[128,3072]{1,0:T(8,128)(2,1)S(1)}, u32[]{:S(2)}, u32[]{:S(2)}) collective-permute-start(bf16[128,3072]{1,0:T(8,128)(2,1)S(1)} %get-tuple-element.138), channel_id=1, source_target_pairs={{16,24},{8,0},{17,25},{9,1},{18,26},{10,2},{19,27},{11,3},{20,28},... | collective-permute-start | bytes 2359304 | tf_op jit(solution)/shard_map/ppermute | solution.py:345
  67.9 27.0 %collective-permute-start.17 = (bf16[64,3072]{1,0:T(8,128)(2,1)S(1)}, bf16[64,3072]{1,0:T(8,128)(2,1)S(1)}, u32[]{:S(2)}, u32[]{:S(2)}) collective-permute-start(bf16[64,3072]{1,0:T(8,128)(2,1)S(1)} %get-tuple-element.151.refs_0_.refs_6_), channel_id=1, source_target_pairs={{0,1},{1,0},{2,3},{3,2},{4,5},{5,4},{6,7},{7,6},{8,9},{9,8},{10,11... | collective-permute-start | bytes 1179656 | tf_op jit(solution)/shard_map/ppermute | solution.py:379
  72.4 23.8 %collective-permute-start.18 = (bf16[64,3072]{1,0:T(8,128)(2,1)S(1)}, bf16[64,3072]{1,0:T(8,128)(2,1)S(1)}, u32[]{:S(2)}, u32[]{:S(2)}) collective-permute-start(bf16[64,3072]{1,0:T(8,128)(2,1)S(1)} %get-tuple-element.152.refs_2_.refs_8_), channel_id=1, source_target_pairs={{0,1},{1,0},{2,3},{3,2},{4,5},{5,4},{6,7},{7,6},{8,9},{9,8},{10,11... | collective-permute-start | bytes 1179656 | tf_op jit(solution)/shard_map/ppermute | solution.py:379
  74.2 22.0 %collective-permute-start.19 = (bf16[64,3072]{1,0:T(8,128)(2,1)S(1)}, bf16[64,3072]{1,0:T(8,128)(2,1)S(1)}, u32[]{:S(2)}, u32[]{:S(2)}) collective-permute-start(bf16[64,3072]{1,0:T(8,128)(2,1)S(1)} %get-tuple-element.153), channel_id=1, source_target_pairs={{0,1},{1,0},{2,3},{3,2},{4,5},{5,4},{6,7},{7,6},{8,9},{9,8},{10,11... | collective-permute-start | bytes 1179656 | tf_op jit(solution)/shard_map/ppermute | solution.py:379
  83.4 33.6 %collective-permute-start.16 = (bf16[128,3072]{1,0:T(8,128)(2,1)S(1)}, bf16[128,3072]{1,0:T(8,128)(2,1)S(1)}, u32[]{:S(2)}, u32[]{:S(2)}) collective-permute-start(bf16[128,3072]{1,0:T(8,128)(2,1)S(1)} %get-tuple-element.150.refs_0_), channel_id=1, source_target_pairs={{0,8},{24,16},{1,9},{25,17},{2,10},{26,18},{3,11},{27,19},{4,12},{... | collective-permute-start | bytes 2359304 | tf_op jit(solution)/shard_map/ppermute | solution.py:345
  91.5 26.7 %collective-permute-start.15 = (bf16[128,3072]{1,0:T(8,128)(2,1)}, bf16[128,3072]{1,0:T(8,128)(2,1)S(1)}, u32[]{:S(2)}, u32[]{:S(2)}) collective-permute-start(bf16[128,3072]{1,0:T(8,128)(2,1)} %get-tuple-element.149), channel_id=1, source_target_pairs={{8,16},{16,8},{9,17},{17,9},{10,18},{18,10},{11,19},{19,11},{12,20... | collective-permute-start | bytes 2359304 | tf_op jit(solution)/shard_map/ppermute | solution.py:345
  94.9 25.0 %collective-permute-start.23 = (bf16[128,3072]{1,0:T(8,128)(2,1)}, bf16[128,3072]{1,0:T(8,128)(2,1)S(1)}, u32[]{:S(2)}, u32[]{:S(2)}) collective-permute-start(bf16[128,3072]{1,0:T(8,128)(2,1)} %get-tuple-element.161), channel_id=1, source_target_pairs={{16,24},{8,0},{17,25},{9,1},{18,26},{10,2},{19,27},{11,3},{20,28},... | collective-permute-start | bytes 2359304 | tf_op jit(solution)/shard_map/ppermute | solution.py:345
  112.9 19.5 %collective-permute-start.22 = (bf16[128,3072]{1,0:T(8,128)(2,1)S(1)}, bf16[128,3072]{1,0:T(8,128)(2,1)S(1)}, u32[]{:S(2)}, u32[]{:S(2)}) collective-permute-start(bf16[128,3072]{1,0:T(8,128)(2,1)S(1)} %get-tuple-element.159.refs_0_), channel_id=1, source_target_pairs={{0,8},{24,16},{1,9},{25,17},{2,10},{26,18},{3,11},{27,19},{4,12},{... | collective-permute-start | bytes 2359304 | tf_op jit(solution)/shard_map/ppermute | solution.py:345
  124.7 24.6 %collective-permute-start.26 = (bf16[128,3072]{1,0:T(8,128)(2,1)S(1)}, bf16[128,3072]{1,0:T(8,128)(2,1)S(1)}, u32[]{:S(2)}, u32[]{:S(2)}) collective-permute-start(bf16[128,3072]{1,0:T(8,128)(2,1)S(1)} %get-tuple-element.171.refs_0_), channel_id=1, source_target_pairs={{0,8},{24,16},{1,9},{25,17},{2,10},{26,18},{3,11},{27,19},{4,12},{... | collective-permute-start | bytes 2359304 | tf_op jit(solution)/shard_map/ppermute | solution.py:345
  134.0 20.0 %collective-permute-start.24 = (bf16[128,3072]{1,0:T(8,128)(2,1)S(1)}, bf16[128,3072]{1,0:T(8,128)(2,1)S(1)}, u32[]{:S(2)}, u32[]{:S(2)}) collective-permute-start(bf16[128,3072]{1,0:T(8,128)(2,1)S(1)} %get-tuple-element.169), channel_id=1, source_target_pairs={{16,24},{8,0},{17,25},{9,1},{18,26},{10,2},{19,27},{11,3},{20,28},... | collective-permute-start | bytes 2359304 | tf_op jit(solution)/shard_map/ppermute | solution.py:345
  140.9 30.7 %collective-permute-start.29 = (bf16[128,3072]{1,0:T(8,128)(2,1)S(1)}, bf16[128,3072]{1,0:T(8,128)(2,1)S(1)}, u32[]{:S(2)}, u32[]{:S(2)}) collective-permute-start(bf16[128,3072]{1,0:T(8,128)(2,1)S(1)} %get-tuple-element.185.refs_0_), channel_id=1, source_target_pairs={{0,8},{24,16},{1,9},{25,17},{2,10},{26,18},{3,11},{27,19},{4,12},{... | collective-permute-start | bytes 2359304 | tf_op jit(solution)/shard_map/ppermute | solution.py:345
  150.5 22.5 %collective-permute-start.28 = (bf16[128,3072]{1,0:T(8,128)(2,1)}, bf16[128,3072]{1,0:T(8,128)(2,1)S(1)}, u32[]{:S(2)}, u32[]{:S(2)}) collective-permute-start(bf16[128,3072]{1,0:T(8,128)(2,1)} %get-tuple-element.184), channel_id=1, source_target_pairs={{8,16},{16,8},{9,17},{17,9},{10,18},{18,10},{11,19},{19,11},{12,20... | collective-permute-start | bytes 2359304 | tf_op jit(solution)/shard_map/ppermute | solution.py:345
  152.5 21.8 %collective-permute-start.27 = (bf16[128,3072]{1,0:T(8,128)(2,1)}, bf16[128,3072]{1,0:T(8,128)(2,1)S(1)}, u32[]{:S(2)}, u32[]{:S(2)}) collective-permute-start(bf16[128,3072]{1,0:T(8,128)(2,1)} %get-tuple-element.182), channel_id=1, source_target_pairs={{16,24},{8,0},{17,25},{9,1},{18,26},{10,2},{19,27},{11,3},{20,28},... | collective-permute-start | bytes 2359304 | tf_op jit(solution)/shard_map/ppermute | solution.py:345
  178.4 28.5 %collective-permute-start.30 = (bf16[256,3072]{1,0:T(8,128)(2,1)}, bf16[256,3072]{1,0:T(8,128)(2,1)S(1)}, u32[]{:S(2)}, u32[]{:S(2)}) collective-permute-start(bf16[256,3072]{1,0:T(8,128)(2,1)} %get-tuple-element.190), channel_id=1, source_target_pairs={{0,1},{1,0},{2,3},{3,2},{4,5},{5,4},{6,7},{7,6},{8,9},{9,8},{10,11... | collective-permute-start | bytes 4718600 | tf_op jit(solution)/shard_map/ppermute | solution.py:379
  182.9 26.3 %collective-permute-start.33 = (bf16[128,3072]{1,0:T(8,128)(2,1)S(1)}, bf16[128,3072]{1,0:T(8,128)(2,1)S(1)}, u32[]{:S(2)}, u32[]{:S(2)}) collective-permute-start(bf16[128,3072]{1,0:T(8,128)(2,1)S(1)} %get-tuple-element.198.refs_0_), channel_id=1, source_target_pairs={{0,8},{24,16},{1,9},{25,17},{2,10},{26,18},{3,11},{27,19},{4,12},{... | collective-permute-start | bytes 2359304 | tf_op jit(solution)/shard_map/ppermute | solution.py:345
  189.5 20.1 %collective-permute-start.32 = (bf16[128,3072]{1,0:T(8,128)(2,1)}, bf16[128,3072]{1,0:T(8,128)(2,1)S(1)}, u32[]{:S(2)}, u32[]{:S(2)}) collective-permute-start(bf16[128,3072]{1,0:T(8,128)(2,1)} %get-tuple-element.197), channel_id=1, source_target_pairs={{8,16},{16,8},{9,17},{17,9},{10,18},{18,10},{11,19},{19,11},{12,20... | collective-permute-start | bytes 2359304 | tf_op jit(solution)/shard_map/ppermute | solution.py:345
  190.2 20.9 %collective-permute-start.31 = (bf16[128,3072]{1,0:T(8,128)(2,1)}, bf16[128,3072]{1,0:T(8,128)(2,1)S(1)}, u32[]{:S(2)}, u32[]{:S(2)}) collective-permute-start(bf16[128,3072]{1,0:T(8,128)(2,1)} %get-tuple-element.195), channel_id=1, source_target_pairs={{16,24},{8,0},{17,25},{9,1},{18,26},{10,2},{19,27},{11,3},{20,28},... | collective-permute-start | bytes 2359304 | tf_op jit(solution)/shard_map/ppermute | solution.py:345
  216.6 20.1 %collective-permute-start.36 = (bf16[128,3072]{1,0:T(8,128)(2,1)S(1)}, bf16[128,3072]{1,0:T(8,128)(2,1)S(1)}, u32[]{:S(2)}, u32[]{:S(2)}) collective-permute-start(bf16[128,3072]{1,0:T(8,128)(2,1)S(1)} %get-tuple-element.212), channel_id=1, source_target_pairs={{16,24},{8,0},{17,25},{9,1},{18,26},{10,2},{19,27},{11,3},{20,28},... | collective-permute-start | bytes 2359304 | tf_op jit(solution)/shard_map/ppermute | solution.py:345
  234.2 20.8 %collective-permute-start.39 = (bf16[128,3072]{1,0:T(8,128)(2,1)S(1)}, bf16[128,3072]{1,0:T(8,128)(2,1)S(1)}, u32[]{:S(2)}, u32[]{:S(2)}) collective-permute-start(bf16[128,3072]{1,0:T(8,128)(2,1)S(1)} %get-tuple-element.224), channel_id=1, source_target_pairs={{16,24},{8,0},{17,25},{9,1},{18,26},{10,2},{19,27},{11,3},{20,28},... | collective-permute-start | bytes 2359304 | tf_op jit(solution)/shard_map/ppermute | solution.py:345
  252.1 33.4 %collective-permute-start.42 = (bf16[64,3072]{1,0:T(8,128)(2,1)S(1)}, bf16[64,3072]{1,0:T(8,128)(2,1)S(1)}, u32[]{:S(2)}, u32[]{:S(2)}) collective-permute-start(bf16[64,3072]{1,0:T(8,128)(2,1)S(1)} %get-tuple-element.234), channel_id=1, source_target_pairs={{0,2},{1,3},{2,0},{3,1},{4,6},{5,7},{6,4},{7,5},{8,10},{9,11},{10,... | collective-permute-start | bytes 1179656 | tf_op jit(solution)/shard_map/ppermute | solution.py:379
  252.6 32.9 %collective-permute-start.43 = (bf16[64,3072]{1,0:T(8,128)(2,1)S(1)}, bf16[64,3072]{1,0:T(8,128)(2,1)S(1)}, u32[]{:S(2)}, u32[]{:S(2)}) collective-permute-start(bf16[64,3072]{1,0:T(8,128)(2,1)S(1)} %get-tuple-element.235), channel_id=1, source_target_pairs={{0,4},{1,5},{2,6},{3,7},{4,0},{5,1},{6,2},{7,3},{8,12},{9,13},{10,... | collective-permute-start | bytes 1179656 | tf_op jit(solution)/shard_map/ppermute | solution.py:379
  256.7 28.8 %collective-permute-start.44 = (bf16[64,3072]{1,0:T(8,128)(2,1)S(1)}, bf16[64,3072]{1,0:T(8,128)(2,1)S(1)}, u32[]{:S(2)}, u32[]{:S(2)}) collective-permute-start(bf16[64,3072]{1,0:T(8,128)(2,1)S(1)} %get-tuple-element.236), channel_id=1, source_target_pairs={{0,6},{1,7},{2,4},{3,5},{4,2},{5,3},{6,0},{7,1},{8,14},{9,15},{10,... | collective-permute-start | bytes 1179656 | tf_op jit(solution)/shard_map/ppermute | solution.py:379
  (68 other events, 1248.2 us)

commit v3 on v2

--- a/solution.py
+++ b/solution.py
@@ -13,7 +13,7 @@
 TILE = 512
 ROW_STEP = 16
 SLOTS = 4
-MATMUL_VMEM = 48 * 1024 * 1024
+MATMUL_VMEM = 36 * 1024 * 1024
 SUM_VMEM = 14 * 1024 * 1024
 COST_STEP = 3500000
 GELU_A = 0.7978845608
@@ -413,18 +413,25 @@
 
         return run
 
-    def work_out(passing=()):
-        pieces = [shard_of(hidden, offset) for offset in halving(n_col)]
-        half = share * n_col // 2
-        results["keep"], results["give"], *passed = order.times_weight(
-            pieces, down_weight, down_mask, [half, half], False, passing
-        )
-        results["bit"] = 1
-        return passed
+    def work_out(chunks):
+        def run(passing=()):
+            chosen = [offset for offset in halving(n_col) if offset // 2 in chunks]
+            half = share * len(chosen) // 2
+            pieces = [shard_of(hidden, offset) for offset in chosen]
+            keep, give, *passed = order.times_weight(pieces, down_weight, down_mask, [half, half], False, passing)
+            results.setdefault("keeps", []).append(keep)
+            results.setdefault("gives", []).append(give)
+            results["bit"] = 1
+            return passed
+
+        return run
 
     def give_out():
-        (give,) = order.tied([results["give"]])
-        results["got"] = swap(give, results["bit"])
+        if results["bit"] == 1:
+            results["keep"], results["give"] = order.stacked(results["keeps"]), order.stacked(results["gives"])
+        else:
+            (results["give"],) = order.tied([results["give"]])
+        results["got"] = swap(results["give"], results["bit"])
 
     def halve_out(passing=()):
         rows = results["keep"].shape[0]
@@ -482,7 +489,8 @@
     work[1].append(partial("a", list(range(3, chips))))
     work[2].append(partial("b", list(range(1, chips)) + [0]))
     last_a = ready(("a", chips - 1))
-    work[last_a].append(work_out)
+    work[last_a - 1].append(work_out(list(range(chips - 1))))
+    work[last_a].append(work_out([chips - 1]))
     work[last_a + 1].append(work_down)
     held = []
     for chunk in range(1, chips):

time: 289 us -> 274 us (0.948)
  local copies, waits for them, and re-layouts: 16.4 us -> 1.81 us
  waiting for transfers between devices: 42.4 us -> 46.4 us
    unnamed x94 -> x12, local copies, waits for them, and re-layouts: 16.4 us -> 1.81 us
    ppermute x24, waiting for transfers between devices: 22.9 us -> 26.7 us  [send(): self.got.append(lax.ppermute(value, 'row', pairs))]
    ppermute x24, starting transfers between devices: 52.1 us -> 48.5 us  [send(): self.got.append(lax.ppermute(value, 'row', pairs))]
    pallas_call x51 -> x52, Pallas kernels: 146 us -> 144 us  [call(): pl.pallas_call(functools.partial(dispatch, kernel, (len(arrays), len(tail...]
  transfers between devices with their start and end apart: 45 -> 45, of which waited for: 13 -> 13; matrix products, arithmetic and copies ran while one was open for 0% -> 0% of each run, Pallas kernels for 49% -> 51%
where the time goes in v3:
time: 274 us; the launch traced here: 273 us
  Pallas kernels  144 us (53%)
  starting transfers between devices  79.2 us (29%)
  waiting for transfers between devices  46.4 us (17%)
    pallas_call x52, Pallas kernels, call(): pl.pallas_call(functools.partial(dispatch, kernel, (len(arrays), len(tail...  144 us
    ppermute x24, starting transfers between devices, send(): self.got.append(lax.ppermute(value, 'row', pairs))  48.5 us
    ppermute x21, starting transfers between devices, swap(): return lax.ppermute(value, 'col', [(i, i ^ offset) for i in range(n_col)])  30.7 us
    ppermute x24, waiting for transfers between devices, send(): self.got.append(lax.ppermute(value, 'row', pairs))  26.7 us
    ppermute x21, waiting for transfers between devices, swap(): return lax.ppermute(value, 'col', [(i, i ^ offset) for i in range(n_col)])  19.8 us
  transfers between devices with their start and end apart: 45, of which 13 were waited for; matrix products, arithmetic and copies ran while one was open for 0% of the time, Pallas kernels for 51%

profile of v3, /device:TPU:1, one launch (start us, length us, event | category | flops | bytes accessed | tf_op | source)
XLA Modules:
  0.0 273.4 jit_solution(18083347870825684458)
XLA Ops:
  7.3 7.6 %shard_map.93 = (bf16[128,3072]{1,0:T(8,128)(2,1)S(1)}, f32[8,128]{1,0:T(8,128)S(1)}) custom-call(bf16[64,3072]{1,0:T(8,128)(2,1)S(1)} %copy-done.1, bf16[64,3072]{1,0:T(8,128)(2,1)S(1)} %collective-permute-done.refs_1_, bf16[3072,3072]{1,0:T(8,128)(2,1)} %refs_2_.9, s32[48,48]{1,0:T(8,128)S(1)} %copy-done.3), custom_call_target="tpu_custom_call" | custom-call | flops 1 | bytes 24500000 | tf_op jit(solution)/shard_map/pallas_call | solution.py:230
  14.9 3.5 %collective-permute-start.1 = (bf16[128,3072]{1,0:T(8,128)(2,1)S(1)}, bf16[128,3072]{1,0:T(8,128)(2,1)S(1)}, u32[]{:S(2)}, u32[]{:S(2)}) collective-permute-start(bf16[128,3072]{1,0:T(8,128)(2,1)S(1)} %get-tuple-element.127.refs_0_), channel_id=1, source_target_pairs={{0,8},{24,16},{1,9},{25,17},{2,10},{26,18},{3,11},{27,19},{4,12},{... | collective-permute-start | bytes 2359304 | tf_op jit(solution)/shard_map/ppermute | solution.py:345
  23.1 9.3 %shard_map.94 = (bf16[128,3072]{1,0:T(8,128)(2,1)S(1)}, bf16[128,3072]{1,0:T(8,128)(2,1)S(1)}, f32[8,128]{1,0:T(8,128)S(1)}) custom-call(bf16[64,3072]{1,0:T(8,128)(2,1)S(1)} %collective-permute-done.2.refs_0_.refs_2_, bf16[64,3072]{1,0:T(8,128)(2,1)S(1)} %collective-permute-done.3.refs_1_.refs_3_, ...), custom_call_target="tpu_custom_call" | custom-call | flops 1 | bytes 33460000 | tf_op jit(solution)/shard_map/pallas_call | solution.py:230
  40.8 3.4 %collective-permute-done.9.refs_1_ = bf16[64,3072]{1,0:T(8,128)(2,1)S(1)} collective-permute-done((bf16[64,3072]{1,0:T(8,128)(2,1)S(1)}, bf16[64,3072]{1,0:T(8,128)(2,1)S(1)}, u32[]{:S(2)}, u32[]{:S(2)}) %collective-permute-start.9) | collective-permute-done | bytes 393248 | tf_op jit(solution)/shard_map/ppermute | solution.py:379
  49.7 5.8 %collective-permute-done.7.refs_1_ = bf16[128,3072]{1,0:T(8,128)(2,1)S(1)} collective-permute-done((bf16[128,3072]{1,0:T(8,128)(2,1)S(1)}, bf16[128,3072]{1,0:T(8,128)(2,1)S(1)}, u32[]{:S(2)}, u32[]{:S(2)}) %collective-permute-start.7) | collective-permute-done | bytes 786464 | tf_op jit(solution)/shard_map/ppermute | solution.py:345
  56.4 6.9 %collective-permute-done.13.refs_0_ = bf16[128,3072]{1,0:T(8,128)(2,1)S(1)} collective-permute-done((bf16[128,3072]{1,0:T(8,128)(2,1)S(1)}, bf16[128,3072]{1,0:T(8,128)(2,1)S(1)}, u32[]{:S(2)}, u32[]{:S(2)}) %collective-permute-start.13) | collective-permute-done | bytes 786464 | tf_op jit(solution)/shard_map/ppermute | solution.py:379
  68.0 4.4 %collective-permute-done.12.refs_1_ = bf16[128,3072]{1,0:T(8,128)(2,1)S(1)} collective-permute-done((bf16[128,3072]{1,0:T(8,128)(2,1)S(1)}, bf16[128,3072]{1,0:T(8,128)(2,1)S(1)}, u32[]{:S(2)}, u32[]{:S(2)}) %collective-permute-start.12) | collective-permute-done | bytes 786464 | tf_op jit(solution)/shard_map/ppermute | solution.py:345
  74.2 7.6 %shard_map.104 = (bf16[128,3072]{1,0:T(8,128)(2,1)S(1)}, f32[8,128]{1,0:T(8,128)S(1)}) custom-call(bf16[128,3072]{1,0:T(8,128)(2,1)S(1)} %get-tuple-element.147.refs_0_.refs_4_.refs_10_.refs_6_, bf16[128,3072]{1,0:T(8,128)(2,1)S(1)} %collective-permute-done.14.refs_1_.refs_5_.refs_11_.refs_7_, bf16[3072,3072]{1,0:T(8,128)(2,1)} %refs_2_.9, ...), custom_call_target="tpu_custom_call" | custom-call | flops 1 | bytes 24500000 | tf_op jit(solution)/shard_map/pallas_call | solution.py:230
  81.8 8.4 %collective-permute-start.16 = (bf16[128,3072]{1,0:T(8,128)(2,1)S(1)}, bf16[128,3072]{1,0:T(8,128)(2,1)S(1)}, u32[]{:S(2)}, u32[]{:S(2)}) collective-permute-start(bf16[128,3072]{1,0:T(8,128)(2,1)S(1)} %get-tuple-element.154.refs_0_), channel_id=1, source_target_pairs={{0,8},{24,16},{1,9},{25,17},{2,10},{26,18},{3,11},{27,19},{4,12},{... | collective-permute-start | bytes 2359304 | tf_op jit(solution)/shard_map/ppermute | solution.py:345
  94.9 14.5 %shard_map.108 = (bf16[128,3072]{1,0:T(8,128)(2,1)S(1)}, bf16[128,3072]{1,0:T(8,128)(2,1)S(1)}, bf16[128,3072]{1,0:T(8,128)(2,1)S(1)}, bf16[128,3072]{1,0:T(8,128)(2,1)S(1)}, f32[8,128]{1,0:T(8,128)S(1)}) custom-call(bf16[64,3072]{1,0:T(8,128)(2,1)S(1)} %get-tuple-element.155.refs_0_.refs_6_, bf16[64,3072]{1,0:T(8,128)(2,1)S(1)} %collective-permute-done.17.refs_1_.refs_7_, ...), custom_call_target="tpu_custom_call" | custom-call | flops 1 | bytes 51380000 | tf_op jit(solution)/shard_map/pallas_call | solution.py:230
  109.4 4.1 %collective-permute-start.22 = (bf16[128,3072]{1,0:T(8,128)(2,1)S(1)}, bf16[128,3072]{1,0:T(8,128)(2,1)S(1)}, u32[]{:S(2)}, u32[]{:S(2)}) collective-permute-start(bf16[128,3072]{1,0:T(8,128)(2,1)S(1)} %get-tuple-element.163.refs_0_), channel_id=1, source_target_pairs={{0,8},{24,16},{1,9},{25,17},{2,10},{26,18},{3,11},{27,19},{4,12},{... | collective-permute-start | bytes 2359304 | tf_op jit(solution)/shard_map/ppermute | solution.py:345
  118.2 4.1 %collective-permute-start.26 = (bf16[128,3072]{1,0:T(8,128)(2,1)S(1)}, bf16[128,3072]{1,0:T(8,128)(2,1)S(1)}, u32[]{:S(2)}, u32[]{:S(2)}) collective-permute-start(bf16[128,3072]{1,0:T(8,128)(2,1)S(1)} %get-tuple-element.178.refs_0_), channel_id=1, source_target_pairs={{0,8},{24,16},{1,9},{25,17},{2,10},{26,18},{3,11},{27,19},{4,12},{... | collective-permute-start | bytes 2359304 | tf_op jit(solution)/shard_map/ppermute | solution.py:345
  122.3 6.6 %collective-permute-done.22.refs_1_ = bf16[128,3072]{1,0:T(8,128)(2,1)S(1)} collective-permute-done((bf16[128,3072]{1,0:T(8,128)(2,1)S(1)}, bf16[128,3072]{1,0:T(8,128)(2,1)S(1)}, u32[]{:S(2)}, u32[]{:S(2)}) %collective-permute-start.22) | collective-permute-done | bytes 786464 | tf_op jit(solution)/shard_map/ppermute | solution.py:345
  136.2 11.7 %shard_map.116 = (bf16[192,3072]{1,0:T(8,128)(2,1)S(1)}, bf16[192,3072]{1,0:T(8,128)(2,1)S(1)}, bf16[128,3072]{1,0:T(8,128)(2,1)S(1)}, f32[8,128]{1,0:T(8,128)S(1)}) custom-call(bf16[128,3072]{1,0:T(8,128)(2,1)S(1)} %get-tuple-element.152.refs_0_.refs_3_, ...), custom_call_target="tpu_custom_call", output_to_operand_aliasing={{2}: (8, {})} | custom-call | flops 1 | bytes 42420000 | tf_op jit(solution)/shard_map/pallas_call | solution.py:230
  147.9 4.1 %collective-permute-start.29 = (bf16[128,3072]{1,0:T(8,128)(2,1)S(1)}, bf16[128,3072]{1,0:T(8,128)(2,1)S(1)}, u32[]{:S(2)}, u32[]{:S(2)}) collective-permute-start(bf16[128,3072]{1,0:T(8,128)(2,1)S(1)} %get-tuple-element.189.refs_0_), channel_id=1, source_target_pairs={{0,8},{24,16},{1,9},{25,17},{2,10},{26,18},{3,11},{27,19},{4,12},{... | collective-permute-start | bytes 2359304 | tf_op jit(solution)/shard_map/ppermute | solution.py:345
  157.0 7.6 %shard_map.120 = (bf16[64,3072]{1,0:T(8,128)(2,1)S(1)}, bf16[64,3072]{1,0:T(8,128)(2,1)S(1)}, bf16[128,3072]{1,0:T(8,128)(2,1)S(1)}, f32[8,128]{1,0:T(8,128)S(1)}) custom-call(bf16[128,3072]{1,0:T(8,128)(2,1)S(1)} %get-tuple-element.182.refs_0_.refs_1_.refs_3_, ...), custom_call_target="tpu_custom_call", output_to_operand_aliasing={{2}: (4, {})} | custom-call | flops 1 | bytes 24500000 | tf_op jit(solution)/shard_map/pallas_call | solution.py:230
  166.3 3.6 %collective-permute-done.27.refs_3_ = bf16[128,3072]{1,0:T(8,128)(2,1)S(1)} collective-permute-done((bf16[128,3072]{1,0:T(8,128)(2,1)S(1)}, bf16[128,3072]{1,0:T(8,128)(2,1)S(1)}, u32[]{:S(2)}, u32[]{:S(2)}) %collective-permute-start.27) | collective-permute-done | bytes 786464 | tf_op jit(solution)/shard_map/ppermute | solution.py:345
  171.8 5.7 %collective-permute-start.30 = (bf16[256,3072]{1,0:T(8,128)(2,1)S(1)}, bf16[256,3072]{1,0:T(8,128)(2,1)S(1)}, u32[]{:S(2)}, u32[]{:S(2)}) collective-permute-start(bf16[256,3072]{1,0:T(8,128)(2,1)S(1)} %get-tuple-element.198), channel_id=1, source_target_pairs={{0,1},{1,0},{2,3},{3,2},{4,5},{5,4},{6,7},{7,6},{8,9},{9,8},{10,11... | collective-permute-start | bytes 4718600 | tf_op jit(solution)/shard_map/ppermute | solution.py:379
  180.9 14.6 %shard_map.126 = (bf16[3072,3072]{1,0:T(8,128)(2,1)}, f32[8,128]{1,0:T(8,128)S(1)}) custom-call(bf16[128,3072]{1,0:T(8,128)(2,1)S(1)} %get-tuple-element.152.refs_0_.refs_3_, bf16[128,3072]{1,0:T(8,128)(2,1)S(1)} %get-tuple-element.172.refs_2_.refs_5_.refs_1_, bf16[128,3072]{1,0:T(8,128)(2,1)S(1)} %get-tuple-element.171.refs_1_.refs_4_.refs_2_, ...), custom_call_target="tpu_custom_call" | custom-call | flops 1 | bytes 52500000 | tf_op jit(solution)/shard_map/pallas_call | solution.py:230
  204.9 9.2 %shard_map.132 = (bf16[128,3072]{1,0:T(8,128)(2,1)S(1)}, bf16[128,3072]{1,0:T(8,128)(2,1)S(1)}, f32[8,128]{1,0:T(8,128)S(1)}) custom-call(bf16[128,3072]{1,0:T(8,128)(2,1)S(1)} %get-tuple-element.212.refs_0_.refs_2_.refs_9_, bf16[128,3072]{1,0:T(8,128)(2,1)S(1)} %get-tuple-element.213.refs_1_.refs_3_.refs_10_, ...), custom_call_target="tpu_custom_call" | custom-call | flops 1 | bytes 33460000 | tf_op jit(solution)/shard_map/pallas_call | solution.py:230
  215.6 3.8 %collective-permute-done.34.refs_1_ = bf16[128,3072]{1,0:T(8,128)(2,1)S(1)} collective-permute-done((bf16[128,3072]{1,0:T(8,128)(2,1)S(1)}, bf16[128,3072]{1,0:T(8,128)(2,1)S(1)}, u32[]{:S(2)}, u32[]{:S(2)}) %collective-permute-start.34) | collective-permute-done | bytes 786464 | tf_op jit(solution)/shard_map/ppermute | solution.py:379
  225.8 10.0 %shard_map.138 = (bf16[64,3072]{1,0:T(8,128)(2,1)S(1)}, bf16[64,3072]{1,0:T(8,128)(2,1)S(1)}, f32[8,128]{1,0:T(8,128)S(1)}) custom-call(bf16[128,3072]{1,0:T(8,128)(2,1)S(1)} %get-tuple-element.228.refs_0_.refs_1_.refs_11_, bf16[128,3072]{1,0:T(8,128)(2,1)S(1)} %get-tuple-element.228.refs_0_.refs_1_.refs_11_, bf16[3072,3072]{1,0:T(8,128)(2,1)} %refs_2_.9, ...), custom_call_target="tpu_custom_call" | custom-call | flops 1 | bytes 24500000 | tf_op jit(solution)/shard_map/pallas_call | solution.py:230
  244.2 10.0 %shard_map.142 = (bf16[64,3072]{1,0:T(8,128)(2,1)S(1)}, bf16[64,3072]{1,0:T(8,128)(2,1)S(1)}, f32[8,128]{1,0:T(8,128)S(1)}) custom-call(bf16[128,3072]{1,0:T(8,128)(2,1)S(1)} %get-tuple-element.235.refs_0_.refs_1_.refs_8_, bf16[128,3072]{1,0:T(8,128)(2,1)S(1)} %get-tuple-element.235.refs_0_.refs_1_.refs_8_, bf16[3072,3072]{1,0:T(8,128)(2,1)} %refs_2_.9, ...), custom_call_target="tpu_custom_call" | custom-call | flops 1 | bytes 24500000 | tf_op jit(solution)/shard_map/pallas_call | solution.py:230
  256.6 14.6 %shard_map.143 = (bf16[3072,3072]{1,0:T(8,128)(2,1)}, f32[8,128]{1,0:T(8,128)S(1)}) custom-call(bf16[64,3072]{1,0:T(8,128)(2,1)S(1)} %copy-done.2, bf16[64,3072]{1,0:T(8,128)(2,1)S(1)} %collective-permute-done.refs_1_, bf16[64,3072]{1,0:T(8,128)(2,1)S(1)} %collective-permute-done.2.refs_0_.refs_2_, ...), custom_call_target="tpu_custom_call" | custom-call | flops 1 | bytes 52500000 | tf_op jit(solution)/shard_map/pallas_call | solution.py:230
  (130 shorter events, 90.7 us)
Async XLA Ops:
  14.9 24.8 %collective-permute-start.1 = (bf16[128,3072]{1,0:T(8,128)(2,1)S(1)}, bf16[128,3072]{1,0:T(8,128)(2,1)S(1)}, u32[]{:S(2)}, u32[]{:S(2)}) collective-permute-start(bf16[128,3072]{1,0:T(8,128)(2,1)S(1)} %get-tuple-element.127.refs_0_), channel_id=1, source_target_pairs={{0,8},{24,16},{1,9},{25,17},{2,10},{26,18},{3,11},{27,19},{4,12},{... | collective-permute-start | bytes 2359304 | tf_op jit(solution)/shard_map/ppermute | solution.py:345
  36.4 19.2 %collective-permute-start.7 = (bf16[128,3072]{1,0:T(8,128)(2,1)S(1)}, bf16[128,3072]{1,0:T(8,128)(2,1)S(1)}, u32[]{:S(2)}, u32[]{:S(2)}) collective-permute-start(bf16[128,3072]{1,0:T(8,128)(2,1)S(1)} %get-tuple-element.133.refs_0_), channel_id=1, source_target_pairs={{0,8},{24,16},{1,9},{25,17},{2,10},{26,18},{3,11},{27,19},{4,12},{... | collective-permute-start | bytes 2359304 | tf_op jit(solution)/shard_map/ppermute | solution.py:345
  45.1 18.3 %collective-permute-start.13 = (bf16[128,3072]{1,0:T(8,128)(2,1)S(1)}, bf16[128,3072]{1,0:T(8,128)(2,1)S(1)}, u32[]{:S(2)}, u32[]{:S(2)}) collective-permute-start(bf16[128,3072]{1,0:T(8,128)(2,1)S(1)} %get-tuple-element.145), channel_id=1, source_target_pairs={{0,6},{1,7},{2,4},{3,5},{4,2},{5,3},{6,0},{7,1},{8,14},{9,15},{10,... | collective-permute-start | bytes 2359304 | tf_op jit(solution)/shard_map/ppermute | solution.py:379
  46.4 26.0 %collective-permute-start.12 = (bf16[128,3072]{1,0:T(8,128)(2,1)S(1)}, bf16[128,3072]{1,0:T(8,128)(2,1)S(1)}, u32[]{:S(2)}, u32[]{:S(2)}) collective-permute-start(bf16[128,3072]{1,0:T(8,128)(2,1)S(1)} %get-tuple-element.144.refs_0_), channel_id=1, source_target_pairs={{0,8},{24,16},{1,9},{25,17},{2,10},{26,18},{3,11},{27,19},{4,12},{... | collective-permute-start | bytes 2359304 | tf_op jit(solution)/shard_map/ppermute | solution.py:345
  66.6 24.0 %collective-permute-start.10 = (bf16[128,3072]{1,0:T(8,128)(2,1)S(1)}, bf16[128,3072]{1,0:T(8,128)(2,1)S(1)}, u32[]{:S(2)}, u32[]{:S(2)}) collective-permute-start(bf16[128,3072]{1,0:T(8,128)(2,1)S(1)} %get-tuple-element.142), channel_id=1, source_target_pairs={{16,24},{8,0},{17,25},{9,1},{18,26},{10,2},{19,27},{11,3},{20,28},... | collective-permute-start | bytes 2359304 | tf_op jit(solution)/shard_map/ppermute | solution.py:345
  67.9 25.7 %collective-permute-start.17 = (bf16[64,3072]{1,0:T(8,128)(2,1)S(1)}, bf16[64,3072]{1,0:T(8,128)(2,1)S(1)}, u32[]{:S(2)}, u32[]{:S(2)}) collective-permute-start(bf16[64,3072]{1,0:T(8,128)(2,1)S(1)} %get-tuple-element.155.refs_0_.refs_6_), channel_id=1, source_target_pairs={{0,1},{1,0},{2,3},{3,2},{4,5},{5,4},{6,7},{7,6},{8,9},{9,8},{10,11... | collective-permute-start | bytes 1179656 | tf_op jit(solution)/shard_map/ppermute | solution.py:379
  72.4 22.5 %collective-permute-start.18 = (bf16[64,3072]{1,0:T(8,128)(2,1)S(1)}, bf16[64,3072]{1,0:T(8,128)(2,1)S(1)}, u32[]{:S(2)}, u32[]{:S(2)}) collective-permute-start(bf16[64,3072]{1,0:T(8,128)(2,1)S(1)} %get-tuple-element.156.refs_2_.refs_8_), channel_id=1, source_target_pairs={{0,1},{1,0},{2,3},{3,2},{4,5},{5,4},{6,7},{7,6},{8,9},{9,8},{10,11... | collective-permute-start | bytes 1179656 | tf_op jit(solution)/shard_map/ppermute | solution.py:379
  74.2 20.7 %collective-permute-start.19 = (bf16[64,3072]{1,0:T(8,128)(2,1)S(1)}, bf16[64,3072]{1,0:T(8,128)(2,1)S(1)}, u32[]{:S(2)}, u32[]{:S(2)}) collective-permute-start(bf16[64,3072]{1,0:T(8,128)(2,1)S(1)} %get-tuple-element.157), channel_id=1, source_target_pairs={{0,1},{1,0},{2,3},{3,2},{4,5},{5,4},{6,7},{7,6},{8,9},{9,8},{10,11... | collective-permute-start | bytes 1179656 | tf_op jit(solution)/shard_map/ppermute | solution.py:379
  81.8 31.7 %collective-permute-start.16 = (bf16[128,3072]{1,0:T(8,128)(2,1)S(1)}, bf16[128,3072]{1,0:T(8,128)(2,1)S(1)}, u32[]{:S(2)}, u32[]{:S(2)}) collective-permute-start(bf16[128,3072]{1,0:T(8,128)(2,1)S(1)} %get-tuple-element.154.refs_0_), channel_id=1, source_target_pairs={{0,8},{24,16},{1,9},{25,17},{2,10},{26,18},{3,11},{27,19},{4,12},{... | collective-permute-start | bytes 2359304 | tf_op jit(solution)/shard_map/ppermute | solution.py:345
  90.7 24.0 %collective-permute-start.15 = (bf16[128,3072]{1,0:T(8,128)(2,1)S(1)}, bf16[128,3072]{1,0:T(8,128)(2,1)S(1)}, u32[]{:S(2)}, u32[]{:S(2)}) collective-permute-start(bf16[128,3072]{1,0:T(8,128)(2,1)S(1)} %get-tuple-element.153), channel_id=1, source_target_pairs={{8,16},{16,8},{9,17},{17,9},{10,18},{18,10},{11,19},{19,11},{12,20... | collective-permute-start | bytes 2359304 | tf_op jit(solution)/shard_map/ppermute | solution.py:345
  93.6 22.8 %collective-permute-start.23 = (bf16[128,3072]{1,0:T(8,128)(2,1)S(1)}, bf16[128,3072]{1,0:T(8,128)(2,1)S(1)}, u32[]{:S(2)}, u32[]{:S(2)}) collective-permute-start(bf16[128,3072]{1,0:T(8,128)(2,1)S(1)} %get-tuple-element.165), channel_id=1, source_target_pairs={{16,24},{8,0},{17,25},{9,1},{18,26},{10,2},{19,27},{11,3},{20,28},... | collective-permute-start | bytes 2359304 | tf_op jit(solution)/shard_map/ppermute | solution.py:345
  109.4 19.5 %collective-permute-start.22 = (bf16[128,3072]{1,0:T(8,128)(2,1)S(1)}, bf16[128,3072]{1,0:T(8,128)(2,1)S(1)}, u32[]{:S(2)}, u32[]{:S(2)}) collective-permute-start(bf16[128,3072]{1,0:T(8,128)(2,1)S(1)} %get-tuple-element.163.refs_0_), channel_id=1, source_target_pairs={{0,8},{24,16},{1,9},{25,17},{2,10},{26,18},{3,11},{27,19},{4,12},{... | collective-permute-start | bytes 2359304 | tf_op jit(solution)/shard_map/ppermute | solution.py:345
  115.1 19.3 %collective-permute-start.20 = (bf16[128,3072]{1,0:T(8,128)(2,1)S(1)}, bf16[128,3072]{1,0:T(8,128)(2,1)S(1)}, u32[]{:S(2)}, u32[]{:S(2)}) collective-permute-start(bf16[128,3072]{1,0:T(8,128)(2,1)S(1)} %get-tuple-element.161), channel_id=1, source_target_pairs={{16,24},{8,0},{17,25},{9,1},{18,26},{10,2},{19,27},{11,3},{20,28},... | collective-permute-start | bytes 2359304 | tf_op jit(solution)/shard_map/ppermute | solution.py:345
  118.2 33.9 %collective-permute-start.26 = (bf16[128,3072]{1,0:T(8,128)(2,1)S(1)}, bf16[128,3072]{1,0:T(8,128)(2,1)S(1)}, u32[]{:S(2)}, u32[]{:S(2)}) collective-permute-start(bf16[128,3072]{1,0:T(8,128)(2,1)S(1)} %get-tuple-element.178.refs_0_), channel_id=1, source_target_pairs={{0,8},{24,16},{1,9},{25,17},{2,10},{26,18},{3,11},{27,19},{4,12},{... | collective-permute-start | bytes 2359304 | tf_op jit(solution)/shard_map/ppermute | solution.py:345
  129.4 23.9 %collective-permute-start.25 = (bf16[128,3072]{1,0:T(8,128)(2,1)S(1)}, bf16[128,3072]{1,0:T(8,128)(2,1)S(1)}, u32[]{:S(2)}, u32[]{:S(2)}) collective-permute-start(bf16[128,3072]{1,0:T(8,128)(2,1)S(1)} %get-tuple-element.177), channel_id=1, source_target_pairs={{8,16},{16,8},{9,17},{17,9},{10,18},{18,10},{11,19},{19,11},{12,20... | collective-permute-start | bytes 2359304 | tf_op jit(solution)/shard_map/ppermute | solution.py:345
  130.5 24.6 %collective-permute-start.24 = (bf16[128,3072]{1,0:T(8,128)(2,1)S(1)}, bf16[128,3072]{1,0:T(8,128)(2,1)S(1)}, u32[]{:S(2)}, u32[]{:S(2)}) collective-permute-start(bf16[128,3072]{1,0:T(8,128)(2,1)S(1)} %get-tuple-element.176), channel_id=1, source_target_pairs={{16,24},{8,0},{17,25},{9,1},{18,26},{10,2},{19,27},{11,3},{20,28},... | collective-permute-start | bytes 2359304 | tf_op jit(solution)/shard_map/ppermute | solution.py:345
  171.8 23.7 %collective-permute-start.30 = (bf16[256,3072]{1,0:T(8,128)(2,1)S(1)}, bf16[256,3072]{1,0:T(8,128)(2,1)S(1)}, u32[]{:S(2)}, u32[]{:S(2)}) collective-permute-start(bf16[256,3072]{1,0:T(8,128)(2,1)S(1)} %get-tuple-element.198), channel_id=1, source_target_pairs={{0,1},{1,0},{2,3},{3,2},{4,5},{5,4},{6,7},{7,6},{8,9},{9,8},{10,11... | collective-permute-start | bytes 4718600 | tf_op jit(solution)/shard_map/ppermute | solution.py:379
  177.5 18.9 %collective-permute-start.33 = (bf16[128,3072]{1,0:T(8,128)(2,1)S(1)}, bf16[128,3072]{1,0:T(8,128)(2,1)S(1)}, u32[]{:S(2)}, u32[]{:S(2)}) collective-permute-start(bf16[128,3072]{1,0:T(8,128)(2,1)S(1)} %get-tuple-element.206.refs_0_), channel_id=1, source_target_pairs={{0,8},{24,16},{1,9},{25,17},{2,10},{26,18},{3,11},{27,19},{4,12},{... | collective-permute-start | bytes 2359304 | tf_op jit(solution)/shard_map/ppermute | solution.py:345
  179.6 20.9 %collective-permute-start.31 = (bf16[128,3072]{1,0:T(8,128)(2,1)}, bf16[128,3072]{1,0:T(8,128)(2,1)S(1)}, u32[]{:S(2)}, u32[]{:S(2)}) collective-permute-start(bf16[128,3072]{1,0:T(8,128)(2,1)} %get-tuple-element.203), channel_id=1, source_target_pairs={{16,24},{8,0},{17,25},{9,1},{18,26},{10,2},{19,27},{11,3},{20,28},... | collective-permute-start | bytes 2359304 | tf_op jit(solution)/shard_map/ppermute | solution.py:345
  203.6 19.5 %collective-permute-start.36 = (bf16[128,3072]{1,0:T(8,128)(2,1)S(1)}, bf16[128,3072]{1,0:T(8,128)(2,1)S(1)}, u32[]{:S(2)}, u32[]{:S(2)}) collective-permute-start(bf16[128,3072]{1,0:T(8,128)(2,1)S(1)} %get-tuple-element.220), channel_id=1, source_target_pairs={{16,24},{8,0},{17,25},{9,1},{18,26},{10,2},{19,27},{11,3},{20,28},... | collective-permute-start | bytes 2359304 | tf_op jit(solution)/shard_map/ppermute | solution.py:345
  221.3 20.5 %collective-permute-start.39 = (bf16[128,3072]{1,0:T(8,128)(2,1)S(1)}, bf16[128,3072]{1,0:T(8,128)(2,1)S(1)}, u32[]{:S(2)}, u32[]{:S(2)}) collective-permute-start(bf16[128,3072]{1,0:T(8,128)(2,1)S(1)} %get-tuple-element.232), channel_id=1, source_target_pairs={{16,24},{8,0},{17,25},{9,1},{18,26},{10,2},{19,27},{11,3},{20,28},... | collective-permute-start | bytes 2359304 | tf_op jit(solution)/shard_map/ppermute | solution.py:345
  238.5 32.7 %collective-permute-start.42 = (bf16[64,3072]{1,0:T(8,128)(2,1)S(1)}, bf16[64,3072]{1,0:T(8,128)(2,1)S(1)}, u32[]{:S(2)}, u32[]{:S(2)}) collective-permute-start(bf16[64,3072]{1,0:T(8,128)(2,1)S(1)} %get-tuple-element.242), channel_id=1, source_target_pairs={{0,2},{1,3},{2,0},{3,1},{4,6},{5,7},{6,4},{7,5},{8,10},{9,11},{10,... | collective-permute-start | bytes 1179656 | tf_op jit(solution)/shard_map/ppermute | solution.py:379
  239.4 31.9 %collective-permute-start.43 = (bf16[64,3072]{1,0:T(8,128)(2,1)S(1)}, bf16[64,3072]{1,0:T(8,128)(2,1)S(1)}, u32[]{:S(2)}, u32[]{:S(2)}) collective-permute-start(bf16[64,3072]{1,0:T(8,128)(2,1)S(1)} %get-tuple-element.243), channel_id=1, source_target_pairs={{0,4},{1,5},{2,6},{3,7},{4,0},{5,1},{6,2},{7,3},{8,12},{9,13},{10,... | collective-permute-start | bytes 1179656 | tf_op jit(solution)/shard_map/ppermute | solution.py:379
  243.5 27.8 %collective-permute-start.44 = (bf16[64,3072]{1,0:T(8,128)(2,1)S(1)}, bf16[64,3072]{1,0:T(8,128)(2,1)S(1)}, u32[]{:S(2)}, u32[]{:S(2)}) collective-permute-start(bf16[64,3072]{1,0:T(8,128)(2,1)S(1)} %get-tuple-element.244), channel_id=1, source_target_pairs={{0,6},{1,7},{2,4},{3,5},{4,2},{5,3},{6,0},{7,1},{8,14},{9,15},{10,... | collective-permute-start | bytes 1179656 | tf_op jit(solution)/shard_map/ppermute | solution.py:379
  (27 other events, 345.8 us)

commit v4 on v3

--- a/solution.py
+++ b/solution.py
@@ -112,12 +112,14 @@
 
 def grad_kernel(x_pieces, g_pieces, scale, tile, refs, tail, out_refs, scratch):
     (mask_hbm,), (out_ref,) = tail, out_refs
-    x_all, g_all, done, mask_ref, out_sems, sems, mask_sem = scratch
+    x_all, x_first, g_all, done, mask_ref, out_sems, sems, first_sems, mask_sem = scratch
     count = len(x_pieces)
-    copies = piece_copies(x_pieces, refs[:count], x_all, sems)
+    later = piece_copies(x_pieces, refs[:count], x_all, sems)
+    columns = [ref.at[:, pl.ds(0, tile)] for ref in refs[:count]]
+    copies = piece_copies(x_pieces, columns, x_first, first_sems)
     copies += piece_copies(g_pieces, refs[count:], g_all, sems.at[pl.ds(count, len(g_pieces))])
     copies.append(pltpu.make_async_copy(mask_hbm, mask_ref, mask_sem))
-    for copy in copies:
+    for copy in copies + later:
         copy.start()
     for copy in copies:
         copy.wait()
@@ -127,24 +129,30 @@
     def leave(step, slot):
         return pltpu.make_async_copy(done.at[slot], out_ref.at[span(step, tile), :], out_sems.at[slot])
 
-    def body(step, carry):
-        slot = lax.rem(step, slots)
-
-        @pl.when(step >= slots)
-        def _():
-            leave(step - slots, slot).wait()
-
+    def rows_done(step, slot, x_tile):
         kept = lane_mask(mask_ref[span(step, blocks), :], width, 0) * scale
         product = lax.dot_general(
-            x_all[:, span(step, tile)], g_all[...], (((0,), (0,)), ((), ())), preferred_element_type=jnp.float32
+            x_tile, g_all[...], (((0,), (0,)), ((), ())), preferred_element_type=jnp.float32
         )
         for block in range(blocks):
             rows = slice(block * BLOCK, (block + 1) * BLOCK)
             done[slot, rows, :] = (product[rows, :] * kept[block : block + 1, :]).astype(done.dtype)
         leave(step, slot).start()
+
+    def body(step, carry):
+        slot = lax.rem(step, slots)
+
+        @pl.when(step >= slots)
+        def _():
+            leave(step - slots, slot).wait()
+
+        rows_done(step, slot, x_all[:, span(step, tile)])
         return carry
 
-    lax.fori_loop(0, steps, body, 0)
+    rows_done(0, 0, x_first[...])
+    for copy in later:
+        copy.wait()
+    lax.fori_loop(1, steps, body, 0)
     for step in range(max(0, steps - slots), steps):
         leave(step, step % slots).wait()
 
@@ -300,11 +308,13 @@
             [jax.ShapeDtypeStruct((depth, width), jnp.bfloat16)],
             [
                 pltpu.VMEM((sum(piece[2] for piece in x_pieces), depth), jnp.bfloat16),
+                pltpu.VMEM((sum(piece[2] for piece in x_pieces), tile), jnp.bfloat16),
                 pltpu.VMEM((sum(piece[2] for piece in g_pieces), width), jnp.bfloat16),
                 pltpu.VMEM((2, tile, width), jnp.bfloat16),
                 pltpu.VMEM(mask.shape, mask.dtype),
                 pltpu.SemaphoreType.DMA((2,)),
                 pltpu.SemaphoreType.DMA((len(pieces),)),
+                pltpu.SemaphoreType.DMA((len(x_pieces),)),
                 pltpu.SemaphoreType.DMA,
             ],
             passing,

time: 274 us -> 274 us (level)
  no operation moved by 1% of the time
where the time goes in v4:
time: 274 us
  Pallas kernels  145 us (53%)
  starting transfers between devices  79.2 us (29%)
  waiting for transfers between devices  46.3 us (17%)
    pallas_call x52, Pallas kernels, call(): pl.pallas_call(functools.partial(dispatch, kernel, (len(arrays), len(tail...  145 us
    ppermute x24, starting transfers between devices, send(): self.got.append(lax.ppermute(value, 'row', pairs))  48.5 us
    ppermute x21, starting transfers between devices, swap(): return lax.ppermute(value, 'col', [(i, i ^ offset) for i in range(n_col)])  30.7 us
    ppermute x24, waiting for transfers between devices, send(): self.got.append(lax.ppermute(value, 'row', pairs))  26.5 us
    ppermute x21, waiting for transfers between devices, swap(): return lax.ppermute(value, 'col', [(i, i ^ offset) for i in range(n_col)])  19.8 us
  transfers between devices with their start and end apart: 45, of which 13 were waited for; matrix products, arithmetic and copies ran while one was open for 0% of the time, Pallas kernels for 51%

profile of v4, /device:TPU:1, one launch (start us, length us, event | category | flops | bytes accessed | tf_op | source)
XLA Modules:
  0.0 273.6 jit_solution(8348573228466297249)
XLA Ops:
  7.3 7.6 %shard_map.93 = (bf16[128,3072]{1,0:T(8,128)(2,1)S(1)}, f32[8,128]{1,0:T(8,128)S(1)}) custom-call(bf16[64,3072]{1,0:T(8,128)(2,1)S(1)} %copy-done.1, bf16[64,3072]{1,0:T(8,128)(2,1)S(1)} %collective-permute-done.refs_1_, bf16[3072,3072]{1,0:T(8,128)(2,1)} %refs_2_.9, s32[48,48]{1,0:T(8,128)S(1)} %copy-done.3), custom_call_target="tpu_custom_call" | custom-call | flops 1 | bytes 24500000 | tf_op jit(solution)/shard_map/pallas_call | solution.py:238
  14.9 3.5 %collective-permute-start.1 = (bf16[128,3072]{1,0:T(8,128)(2,1)S(1)}, bf16[128,3072]{1,0:T(8,128)(2,1)S(1)}, u32[]{:S(2)}, u32[]{:S(2)}) collective-permute-start(bf16[128,3072]{1,0:T(8,128)(2,1)S(1)} %get-tuple-element.127.refs_0_), channel_id=1, source_target_pairs={{0,8},{24,16},{1,9},{25,17},{2,10},{26,18},{3,11},{27,19},{4,12},{... | collective-permute-start | bytes 2359304 | tf_op jit(solution)/shard_map/ppermute | solution.py:355
  23.1 9.3 %shard_map.94 = (bf16[128,3072]{1,0:T(8,128)(2,1)S(1)}, bf16[128,3072]{1,0:T(8,128)(2,1)S(1)}, f32[8,128]{1,0:T(8,128)S(1)}) custom-call(bf16[64,3072]{1,0:T(8,128)(2,1)S(1)} %collective-permute-done.2.refs_0_.refs_2_, bf16[64,3072]{1,0:T(8,128)(2,1)S(1)} %collective-permute-done.3.refs_1_.refs_3_, ...), custom_call_target="tpu_custom_call" | custom-call | flops 1 | bytes 33460000 | tf_op jit(solution)/shard_map/pallas_call | solution.py:238
  40.8 3.4 %collective-permute-done.9.refs_1_ = bf16[64,3072]{1,0:T(8,128)(2,1)S(1)} collective-permute-done((bf16[64,3072]{1,0:T(8,128)(2,1)S(1)}, bf16[64,3072]{1,0:T(8,128)(2,1)S(1)}, u32[]{:S(2)}, u32[]{:S(2)}) %collective-permute-start.9) | collective-permute-done | bytes 393248 | tf_op jit(solution)/shard_map/ppermute | solution.py:389
  49.7 5.8 %collective-permute-done.7.refs_1_ = bf16[128,3072]{1,0:T(8,128)(2,1)S(1)} collective-permute-done((bf16[128,3072]{1,0:T(8,128)(2,1)S(1)}, bf16[128,3072]{1,0:T(8,128)(2,1)S(1)}, u32[]{:S(2)}, u32[]{:S(2)}) %collective-permute-start.7) | collective-permute-done | bytes 786464 | tf_op jit(solution)/shard_map/ppermute | solution.py:355
  56.4 6.9 %collective-permute-done.13.refs_0_ = bf16[128,3072]{1,0:T(8,128)(2,1)S(1)} collective-permute-done((bf16[128,3072]{1,0:T(8,128)(2,1)S(1)}, bf16[128,3072]{1,0:T(8,128)(2,1)S(1)}, u32[]{:S(2)}, u32[]{:S(2)}) %collective-permute-start.13) | collective-permute-done | bytes 786464 | tf_op jit(solution)/shard_map/ppermute | solution.py:389
  68.0 4.4 %collective-permute-done.12.refs_1_ = bf16[128,3072]{1,0:T(8,128)(2,1)S(1)} collective-permute-done((bf16[128,3072]{1,0:T(8,128)(2,1)S(1)}, bf16[128,3072]{1,0:T(8,128)(2,1)S(1)}, u32[]{:S(2)}, u32[]{:S(2)}) %collective-permute-start.12) | collective-permute-done | bytes 786464 | tf_op jit(solution)/shard_map/ppermute | solution.py:355
  74.2 7.6 %shard_map.104 = (bf16[128,3072]{1,0:T(8,128)(2,1)S(1)}, f32[8,128]{1,0:T(8,128)S(1)}) custom-call(bf16[128,3072]{1,0:T(8,128)(2,1)S(1)} %get-tuple-element.147.refs_0_.refs_4_.refs_10_.refs_6_, bf16[128,3072]{1,0:T(8,128)(2,1)S(1)} %collective-permute-done.14.refs_1_.refs_5_.refs_11_.refs_7_, bf16[3072,3072]{1,0:T(8,128)(2,1)} %refs_2_.9, ...), custom_call_target="tpu_custom_call" | custom-call | flops 1 | bytes 24500000 | tf_op jit(solution)/shard_map/pallas_call | solution.py:238
  81.8 8.4 %collective-permute-start.16 = (bf16[128,3072]{1,0:T(8,128)(2,1)S(1)}, bf16[128,3072]{1,0:T(8,128)(2,1)S(1)}, u32[]{:S(2)}, u32[]{:S(2)}) collective-permute-start(bf16[128,3072]{1,0:T(8,128)(2,1)S(1)} %get-tuple-element.154.refs_0_), channel_id=1, source_target_pairs={{0,8},{24,16},{1,9},{25,17},{2,10},{26,18},{3,11},{27,19},{4,12},{... | collective-permute-start | bytes 2359304 | tf_op jit(solution)/shard_map/ppermute | solution.py:355
  94.9 14.5 %shard_map.108 = (bf16[128,3072]{1,0:T(8,128)(2,1)S(1)}, bf16[128,3072]{1,0:T(8,128)(2,1)S(1)}, bf16[128,3072]{1,0:T(8,128)(2,1)S(1)}, bf16[128,3072]{1,0:T(8,128)(2,1)S(1)}, f32[8,128]{1,0:T(8,128)S(1)}) custom-call(bf16[64,3072]{1,0:T(8,128)(2,1)S(1)} %get-tuple-element.155.refs_0_.refs_6_, bf16[64,3072]{1,0:T(8,128)(2,1)S(1)} %collective-permute-done.17.refs_1_.refs_7_, ...), custom_call_target="tpu_custom_call" | custom-call | flops 1 | bytes 51380000 | tf_op jit(solution)/shard_map/pallas_call | solution.py:238
  109.4 4.1 %collective-permute-start.22 = (bf16[128,3072]{1,0:T(8,128)(2,1)S(1)}, bf16[128,3072]{1,0:T(8,128)(2,1)S(1)}, u32[]{:S(2)}, u32[]{:S(2)}) collective-permute-start(bf16[128,3072]{1,0:T(8,128)(2,1)S(1)} %get-tuple-element.163.refs_0_), channel_id=1, source_target_pairs={{0,8},{24,16},{1,9},{25,17},{2,10},{26,18},{3,11},{27,19},{4,12},{... | collective-permute-start | bytes 2359304 | tf_op jit(solution)/shard_map/ppermute | solution.py:355
  118.2 4.1 %collective-permute-start.26 = (bf16[128,3072]{1,0:T(8,128)(2,1)S(1)}, bf16[128,3072]{1,0:T(8,128)(2,1)S(1)}, u32[]{:S(2)}, u32[]{:S(2)}) collective-permute-start(bf16[128,3072]{1,0:T(8,128)(2,1)S(1)} %get-tuple-element.178.refs_0_), channel_id=1, source_target_pairs={{0,8},{24,16},{1,9},{25,17},{2,10},{26,18},{3,11},{27,19},{4,12},{... | collective-permute-start | bytes 2359304 | tf_op jit(solution)/shard_map/ppermute | solution.py:355
  122.3 6.6 %collective-permute-done.22.refs_1_ = bf16[128,3072]{1,0:T(8,128)(2,1)S(1)} collective-permute-done((bf16[128,3072]{1,0:T(8,128)(2,1)S(1)}, bf16[128,3072]{1,0:T(8,128)(2,1)S(1)}, u32[]{:S(2)}, u32[]{:S(2)}) %collective-permute-start.22) | collective-permute-done | bytes 786464 | tf_op jit(solution)/shard_map/ppermute | solution.py:355
  136.2 11.7 %shard_map.116 = (bf16[192,3072]{1,0:T(8,128)(2,1)S(1)}, bf16[192,3072]{1,0:T(8,128)(2,1)S(1)}, bf16[128,3072]{1,0:T(8,128)(2,1)S(1)}, f32[8,128]{1,0:T(8,128)S(1)}) custom-call(bf16[128,3072]{1,0:T(8,128)(2,1)S(1)} %get-tuple-element.152.refs_0_.refs_3_, ...), custom_call_target="tpu_custom_call", output_to_operand_aliasing={{2}: (8, {})} | custom-call | flops 1 | bytes 42420000 | tf_op jit(solution)/shard_map/pallas_call | solution.py:238
  147.9 4.1 %collective-permute-start.29 = (bf16[128,3072]{1,0:T(8,128)(2,1)S(1)}, bf16[128,3072]{1,0:T(8,128)(2,1)S(1)}, u32[]{:S(2)}, u32[]{:S(2)}) collective-permute-start(bf16[128,3072]{1,0:T(8,128)(2,1)S(1)} %get-tuple-element.189.refs_0_), channel_id=1, source_target_pairs={{0,8},{24,16},{1,9},{25,17},{2,10},{26,18},{3,11},{27,19},{4,12},{... | collective-permute-start | bytes 2359304 | tf_op jit(solution)/shard_map/ppermute | solution.py:355
  157.0 7.6 %shard_map.120 = (bf16[64,3072]{1,0:T(8,128)(2,1)S(1)}, bf16[64,3072]{1,0:T(8,128)(2,1)S(1)}, bf16[128,3072]{1,0:T(8,128)(2,1)S(1)}, f32[8,128]{1,0:T(8,128)S(1)}) custom-call(bf16[128,3072]{1,0:T(8,128)(2,1)S(1)} %get-tuple-element.182.refs_0_.refs_1_.refs_3_, ...), custom_call_target="tpu_custom_call", output_to_operand_aliasing={{2}: (4, {})} | custom-call | flops 1 | bytes 24500000 | tf_op jit(solution)/shard_map/pallas_call | solution.py:238
  166.3 3.6 %collective-permute-done.27.refs_3_ = bf16[128,3072]{1,0:T(8,128)(2,1)S(1)} collective-permute-done((bf16[128,3072]{1,0:T(8,128)(2,1)S(1)}, bf16[128,3072]{1,0:T(8,128)(2,1)S(1)}, u32[]{:S(2)}, u32[]{:S(2)}) %collective-permute-start.27) | collective-permute-done | bytes 786464 | tf_op jit(solution)/shard_map/ppermute | solution.py:355
  171.8 5.7 %collective-permute-start.30 = (bf16[256,3072]{1,0:T(8,128)(2,1)S(1)}, bf16[256,3072]{1,0:T(8,128)(2,1)S(1)}, u32[]{:S(2)}, u32[]{:S(2)}) collective-permute-start(bf16[256,3072]{1,0:T(8,128)(2,1)S(1)} %get-tuple-element.198), channel_id=1, source_target_pairs={{0,1},{1,0},{2,3},{3,2},{4,5},{5,4},{6,7},{7,6},{8,9},{9,8},{10,11... | collective-permute-start | bytes 4718600 | tf_op jit(solution)/shard_map/ppermute | solution.py:389
  180.9 14.7 %shard_map.126 = (bf16[3072,3072]{1,0:T(8,128)(2,1)}, f32[8,128]{1,0:T(8,128)S(1)}) custom-call(bf16[128,3072]{1,0:T(8,128)(2,1)S(1)} %get-tuple-element.152.refs_0_.refs_3_, bf16[128,3072]{1,0:T(8,128)(2,1)S(1)} %get-tuple-element.172.refs_2_.refs_5_.refs_1_, bf16[128,3072]{1,0:T(8,128)(2,1)S(1)} %get-tuple-element.171.refs_1_.refs_4_.refs_2_, ...), custom_call_target="tpu_custom_call" | custom-call | flops 1 | bytes 52500000 | tf_op jit(solution)/shard_map/pallas_call | solution.py:238
  204.9 9.2 %shard_map.132 = (bf16[128,3072]{1,0:T(8,128)(2,1)S(1)}, bf16[128,3072]{1,0:T(8,128)(2,1)S(1)}, f32[8,128]{1,0:T(8,128)S(1)}) custom-call(bf16[128,3072]{1,0:T(8,128)(2,1)S(1)} %get-tuple-element.212.refs_0_.refs_2_.refs_9_, bf16[128,3072]{1,0:T(8,128)(2,1)S(1)} %get-tuple-element.213.refs_1_.refs_3_.refs_10_, ...), custom_call_target="tpu_custom_call" | custom-call | flops 1 | bytes 33460000 | tf_op jit(solution)/shard_map/pallas_call | solution.py:238
  215.6 3.8 %collective-permute-done.34.refs_1_ = bf16[128,3072]{1,0:T(8,128)(2,1)S(1)} collective-permute-done((bf16[128,3072]{1,0:T(8,128)(2,1)S(1)}, bf16[128,3072]{1,0:T(8,128)(2,1)S(1)}, u32[]{:S(2)}, u32[]{:S(2)}) %collective-permute-start.34) | collective-permute-done | bytes 786464 | tf_op jit(solution)/shard_map/ppermute | solution.py:389
  225.8 10.0 %shard_map.138 = (bf16[64,3072]{1,0:T(8,128)(2,1)S(1)}, bf16[64,3072]{1,0:T(8,128)(2,1)S(1)}, f32[8,128]{1,0:T(8,128)S(1)}) custom-call(bf16[128,3072]{1,0:T(8,128)(2,1)S(1)} %get-tuple-element.228.refs_0_.refs_1_.refs_11_, bf16[128,3072]{1,0:T(8,128)(2,1)S(1)} %get-tuple-element.228.refs_0_.refs_1_.refs_11_, bf16[3072,3072]{1,0:T(8,128)(2,1)} %refs_2_.9, ...), custom_call_target="tpu_custom_call" | custom-call | flops 1 | bytes 24500000 | tf_op jit(solution)/shard_map/pallas_call | solution.py:238
  244.2 10.0 %shard_map.142 = (bf16[64,3072]{1,0:T(8,128)(2,1)S(1)}, bf16[64,3072]{1,0:T(8,128)(2,1)S(1)}, f32[8,128]{1,0:T(8,128)S(1)}) custom-call(bf16[128,3072]{1,0:T(8,128)(2,1)S(1)} %get-tuple-element.235.refs_0_.refs_1_.refs_8_, bf16[128,3072]{1,0:T(8,128)(2,1)S(1)} %get-tuple-element.235.refs_0_.refs_1_.refs_8_, bf16[3072,3072]{1,0:T(8,128)(2,1)} %refs_2_.9, ...), custom_call_target="tpu_custom_call" | custom-call | flops 1 | bytes 24500000 | tf_op jit(solution)/shard_map/pallas_call | solution.py:238
  256.6 14.8 %shard_map.143 = (bf16[3072,3072]{1,0:T(8,128)(2,1)}, f32[8,128]{1,0:T(8,128)S(1)}) custom-call(bf16[64,3072]{1,0:T(8,128)(2,1)S(1)} %copy-done.2, bf16[64,3072]{1,0:T(8,128)(2,1)S(1)} %collective-permute-done.refs_1_, bf16[64,3072]{1,0:T(8,128)(2,1)S(1)} %collective-permute-done.2.refs_0_.refs_2_, ...), custom_call_target="tpu_custom_call" | custom-call | flops 1 | bytes 52500000 | tf_op jit(solution)/shard_map/pallas_call | solution.py:238
  (130 shorter events, 90.6 us)
Async XLA Ops:
  14.9 24.8 %collective-permute-start.1 = (bf16[128,3072]{1,0:T(8,128)(2,1)S(1)}, bf16[128,3072]{1,0:T(8,128)(2,1)S(1)}, u32[]{:S(2)}, u32[]{:S(2)}) collective-permute-start(bf16[128,3072]{1,0:T(8,128)(2,1)S(1)} %get-tuple-element.127.refs_0_), channel_id=1, source_target_pairs={{0,8},{24,16},{1,9},{25,17},{2,10},{26,18},{3,11},{27,19},{4,12},{... | collective-permute-start | bytes 2359304 | tf_op jit(solution)/shard_map/ppermute | solution.py:355
  36.4 19.2 %collective-permute-start.7 = (bf16[128,3072]{1,0:T(8,128)(2,1)S(1)}, bf16[128,3072]{1,0:T(8,128)(2,1)S(1)}, u32[]{:S(2)}, u32[]{:S(2)}) collective-permute-start(bf16[128,3072]{1,0:T(8,128)(2,1)S(1)} %get-tuple-element.133.refs_0_), channel_id=1, source_target_pairs={{0,8},{24,16},{1,9},{25,17},{2,10},{26,18},{3,11},{27,19},{4,12},{... | collective-permute-start | bytes 2359304 | tf_op jit(solution)/shard_map/ppermute | solution.py:355
  45.1 18.3 %collective-permute-start.13 = (bf16[128,3072]{1,0:T(8,128)(2,1)S(1)}, bf16[128,3072]{1,0:T(8,128)(2,1)S(1)}, u32[]{:S(2)}, u32[]{:S(2)}) collective-permute-start(bf16[128,3072]{1,0:T(8,128)(2,1)S(1)} %get-tuple-element.145), channel_id=1, source_target_pairs={{0,6},{1,7},{2,4},{3,5},{4,2},{5,3},{6,0},{7,1},{8,14},{9,15},{10,... | collective-permute-start | bytes 2359304 | tf_op jit(solution)/shard_map/ppermute | solution.py:389
  46.4 26.0 %collective-permute-start.12 = (bf16[128,3072]{1,0:T(8,128)(2,1)S(1)}, bf16[128,3072]{1,0:T(8,128)(2,1)S(1)}, u32[]{:S(2)}, u32[]{:S(2)}) collective-permute-start(bf16[128,3072]{1,0:T(8,128)(2,1)S(1)} %get-tuple-element.144.refs_0_), channel_id=1, source_target_pairs={{0,8},{24,16},{1,9},{25,17},{2,10},{26,18},{3,11},{27,19},{4,12},{... | collective-permute-start | bytes 2359304 | tf_op jit(solution)/shard_map/ppermute | solution.py:355
  66.6 24.0 %collective-permute-start.10 = (bf16[128,3072]{1,0:T(8,128)(2,1)S(1)}, bf16[128,3072]{1,0:T(8,128)(2,1)S(1)}, u32[]{:S(2)}, u32[]{:S(2)}) collective-permute-start(bf16[128,3072]{1,0:T(8,128)(2,1)S(1)} %get-tuple-element.142), channel_id=1, source_target_pairs={{16,24},{8,0},{17,25},{9,1},{18,26},{10,2},{19,27},{11,3},{20,28},... | collective-permute-start | bytes 2359304 | tf_op jit(solution)/shard_map/ppermute | solution.py:355
  67.9 25.7 %collective-permute-start.17 = (bf16[64,3072]{1,0:T(8,128)(2,1)S(1)}, bf16[64,3072]{1,0:T(8,128)(2,1)S(1)}, u32[]{:S(2)}, u32[]{:S(2)}) collective-permute-start(bf16[64,3072]{1,0:T(8,128)(2,1)S(1)} %get-tuple-element.155.refs_0_.refs_6_), channel_id=1, source_target_pairs={{0,1},{1,0},{2,3},{3,2},{4,5},{5,4},{6,7},{7,6},{8,9},{9,8},{10,11... | collective-permute-start | bytes 1179656 | tf_op jit(solution)/shard_map/ppermute | solution.py:389
  72.4 22.5 %collective-permute-start.18 = (bf16[64,3072]{1,0:T(8,128)(2,1)S(1)}, bf16[64,3072]{1,0:T(8,128)(2,1)S(1)}, u32[]{:S(2)}, u32[]{:S(2)}) collective-permute-start(bf16[64,3072]{1,0:T(8,128)(2,1)S(1)} %get-tuple-element.156.refs_2_.refs_8_), channel_id=1, source_target_pairs={{0,1},{1,0},{2,3},{3,2},{4,5},{5,4},{6,7},{7,6},{8,9},{9,8},{10,11... | collective-permute-start | bytes 1179656 | tf_op jit(solution)/shard_map/ppermute | solution.py:389
  74.2 20.7 %collective-permute-start.19 = (bf16[64,3072]{1,0:T(8,128)(2,1)S(1)}, bf16[64,3072]{1,0:T(8,128)(2,1)S(1)}, u32[]{:S(2)}, u32[]{:S(2)}) collective-permute-start(bf16[64,3072]{1,0:T(8,128)(2,1)S(1)} %get-tuple-element.157), channel_id=1, source_target_pairs={{0,1},{1,0},{2,3},{3,2},{4,5},{5,4},{6,7},{7,6},{8,9},{9,8},{10,11... | collective-permute-start | bytes 1179656 | tf_op jit(solution)/shard_map/ppermute | solution.py:389
  81.8 31.7 %collective-permute-start.16 = (bf16[128,3072]{1,0:T(8,128)(2,1)S(1)}, bf16[128,3072]{1,0:T(8,128)(2,1)S(1)}, u32[]{:S(2)}, u32[]{:S(2)}) collective-permute-start(bf16[128,3072]{1,0:T(8,128)(2,1)S(1)} %get-tuple-element.154.refs_0_), channel_id=1, source_target_pairs={{0,8},{24,16},{1,9},{25,17},{2,10},{26,18},{3,11},{27,19},{4,12},{... | collective-permute-start | bytes 2359304 | tf_op jit(solution)/shard_map/ppermute | solution.py:355
  90.7 24.0 %collective-permute-start.15 = (bf16[128,3072]{1,0:T(8,128)(2,1)S(1)}, bf16[128,3072]{1,0:T(8,128)(2,1)S(1)}, u32[]{:S(2)}, u32[]{:S(2)}) collective-permute-start(bf16[128,3072]{1,0:T(8,128)(2,1)S(1)} %get-tuple-element.153), channel_id=1, source_target_pairs={{8,16},{16,8},{9,17},{17,9},{10,18},{18,10},{11,19},{19,11},{12,20... | collective-permute-start | bytes 2359304 | tf_op jit(solution)/shard_map/ppermute | solution.py:355
  93.6 22.8 %collective-permute-start.23 = (bf16[128,3072]{1,0:T(8,128)(2,1)S(1)}, bf16[128,3072]{1,0:T(8,128)(2,1)S(1)}, u32[]{:S(2)}, u32[]{:S(2)}) collective-permute-start(bf16[128,3072]{1,0:T(8,128)(2,1)S(1)} %get-tuple-element.165), channel_id=1, source_target_pairs={{16,24},{8,0},{17,25},{9,1},{18,26},{10,2},{19,27},{11,3},{20,28},... | collective-permute-start | bytes 2359304 | tf_op jit(solution)/shard_map/ppermute | solution.py:355
  109.4 19.5 %collective-permute-start.22 = (bf16[128,3072]{1,0:T(8,128)(2,1)S(1)}, bf16[128,3072]{1,0:T(8,128)(2,1)S(1)}, u32[]{:S(2)}, u32[]{:S(2)}) collective-permute-start(bf16[128,3072]{1,0:T(8,128)(2,1)S(1)} %get-tuple-element.163.refs_0_), channel_id=1, source_target_pairs={{0,8},{24,16},{1,9},{25,17},{2,10},{26,18},{3,11},{27,19},{4,12},{... | collective-permute-start | bytes 2359304 | tf_op jit(solution)/shard_map/ppermute | solution.py:355
  115.1 19.3 %collective-permute-start.20 = (bf16[128,3072]{1,0:T(8,128)(2,1)S(1)}, bf16[128,3072]{1,0:T(8,128)(2,1)S(1)}, u32[]{:S(2)}, u32[]{:S(2)}) collective-permute-start(bf16[128,3072]{1,0:T(8,128)(2,1)S(1)} %get-tuple-element.161), channel_id=1, source_target_pairs={{16,24},{8,0},{17,25},{9,1},{18,26},{10,2},{19,27},{11,3},{20,28},... | collective-permute-start | bytes 2359304 | tf_op jit(solution)/shard_map/ppermute | solution.py:355
  118.2 33.9 %collective-permute-start.26 = (bf16[128,3072]{1,0:T(8,128)(2,1)S(1)}, bf16[128,3072]{1,0:T(8,128)(2,1)S(1)}, u32[]{:S(2)}, u32[]{:S(2)}) collective-permute-start(bf16[128,3072]{1,0:T(8,128)(2,1)S(1)} %get-tuple-element.178.refs_0_), channel_id=1, source_target_pairs={{0,8},{24,16},{1,9},{25,17},{2,10},{26,18},{3,11},{27,19},{4,12},{... | collective-permute-start | bytes 2359304 | tf_op jit(solution)/shard_map/ppermute | solution.py:355
  129.4 23.9 %collective-permute-start.25 = (bf16[128,3072]{1,0:T(8,128)(2,1)S(1)}, bf16[128,3072]{1,0:T(8,128)(2,1)S(1)}, u32[]{:S(2)}, u32[]{:S(2)}) collective-permute-start(bf16[128,3072]{1,0:T(8,128)(2,1)S(1)} %get-tuple-element.177), channel_id=1, source_target_pairs={{8,16},{16,8},{9,17},{17,9},{10,18},{18,10},{11,19},{19,11},{12,20... | collective-permute-start | bytes 2359304 | tf_op jit(solution)/shard_map/ppermute | solution.py:355
  130.5 24.6 %collective-permute-start.24 = (bf16[128,3072]{1,0:T(8,128)(2,1)S(1)}, bf16[128,3072]{1,0:T(8,128)(2,1)S(1)}, u32[]{:S(2)}, u32[]{:S(2)}) collective-permute-start(bf16[128,3072]{1,0:T(8,128)(2,1)S(1)} %get-tuple-element.176), channel_id=1, source_target_pairs={{16,24},{8,0},{17,25},{9,1},{18,26},{10,2},{19,27},{11,3},{20,28},... | collective-permute-start | bytes 2359304 | tf_op jit(solution)/shard_map/ppermute | solution.py:355
  171.8 23.8 %collective-permute-start.30 = (bf16[256,3072]{1,0:T(8,128)(2,1)S(1)}, bf16[256,3072]{1,0:T(8,128)(2,1)S(1)}, u32[]{:S(2)}, u32[]{:S(2)}) collective-permute-start(bf16[256,3072]{1,0:T(8,128)(2,1)S(1)} %get-tuple-element.198), channel_id=1, source_target_pairs={{0,1},{1,0},{2,3},{3,2},{4,5},{5,4},{6,7},{7,6},{8,9},{9,8},{10,11... | collective-permute-start | bytes 4718600 | tf_op jit(solution)/shard_map/ppermute | solution.py:389
  177.5 19.0 %collective-permute-start.33 = (bf16[128,3072]{1,0:T(8,128)(2,1)S(1)}, bf16[128,3072]{1,0:T(8,128)(2,1)S(1)}, u32[]{:S(2)}, u32[]{:S(2)}) collective-permute-start(bf16[128,3072]{1,0:T(8,128)(2,1)S(1)} %get-tuple-element.206.refs_0_), channel_id=1, source_target_pairs={{0,8},{24,16},{1,9},{25,17},{2,10},{26,18},{3,11},{27,19},{4,12},{... | collective-permute-start | bytes 2359304 | tf_op jit(solution)/shard_map/ppermute | solution.py:355
  179.6 20.9 %collective-permute-start.31 = (bf16[128,3072]{1,0:T(8,128)(2,1)}, bf16[128,3072]{1,0:T(8,128)(2,1)S(1)}, u32[]{:S(2)}, u32[]{:S(2)}) collective-permute-start(bf16[128,3072]{1,0:T(8,128)(2,1)} %get-tuple-element.203), channel_id=1, source_target_pairs={{16,24},{8,0},{17,25},{9,1},{18,26},{10,2},{19,27},{11,3},{20,28},... | collective-permute-start | bytes 2359304 | tf_op jit(solution)/shard_map/ppermute | solution.py:355
  203.6 19.5 %collective-permute-start.36 = (bf16[128,3072]{1,0:T(8,128)(2,1)S(1)}, bf16[128,3072]{1,0:T(8,128)(2,1)S(1)}, u32[]{:S(2)}, u32[]{:S(2)}) collective-permute-start(bf16[128,3072]{1,0:T(8,128)(2,1)S(1)} %get-tuple-element.220), channel_id=1, source_target_pairs={{16,24},{8,0},{17,25},{9,1},{18,26},{10,2},{19,27},{11,3},{20,28},... | collective-permute-start | bytes 2359304 | tf_op jit(solution)/shard_map/ppermute | solution.py:355
  221.3 20.5 %collective-permute-start.39 = (bf16[128,3072]{1,0:T(8,128)(2,1)S(1)}, bf16[128,3072]{1,0:T(8,128)(2,1)S(1)}, u32[]{:S(2)}, u32[]{:S(2)}) collective-permute-start(bf16[128,3072]{1,0:T(8,128)(2,1)S(1)} %get-tuple-element.232), channel_id=1, source_target_pairs={{16,24},{8,0},{17,25},{9,1},{18,26},{10,2},{19,27},{11,3},{20,28},... | collective-permute-start | bytes 2359304 | tf_op jit(solution)/shard_map/ppermute | solution.py:355
  238.5 32.8 %collective-permute-start.42 = (bf16[64,3072]{1,0:T(8,128)(2,1)S(1)}, bf16[64,3072]{1,0:T(8,128)(2,1)S(1)}, u32[]{:S(2)}, u32[]{:S(2)}) collective-permute-start(bf16[64,3072]{1,0:T(8,128)(2,1)S(1)} %get-tuple-element.242), channel_id=1, source_target_pairs={{0,2},{1,3},{2,0},{3,1},{4,6},{5,7},{6,4},{7,5},{8,10},{9,11},{10,... | collective-permute-start | bytes 1179656 | tf_op jit(solution)/shard_map/ppermute | solution.py:389
  239.4 32.0 %collective-permute-start.43 = (bf16[64,3072]{1,0:T(8,128)(2,1)S(1)}, bf16[64,3072]{1,0:T(8,128)(2,1)S(1)}, u32[]{:S(2)}, u32[]{:S(2)}) collective-permute-start(bf16[64,3072]{1,0:T(8,128)(2,1)S(1)} %get-tuple-element.243), channel_id=1, source_target_pairs={{0,4},{1,5},{2,6},{3,7},{4,0},{5,1},{6,2},{7,3},{8,12},{9,13},{10,... | collective-permute-start | bytes 1179656 | tf_op jit(solution)/shard_map/ppermute | solution.py:389
  243.5 27.9 %collective-permute-start.44 = (bf16[64,3072]{1,0:T(8,128)(2,1)S(1)}, bf16[64,3072]{1,0:T(8,128)(2,1)S(1)}, u32[]{:S(2)}, u32[]{:S(2)}) collective-permute-start(bf16[64,3072]{1,0:T(8,128)(2,1)S(1)} %get-tuple-element.244), channel_id=1, source_target_pairs={{0,6},{1,7},{2,4},{3,5},{4,2},{5,3},{6,0},{7,1},{8,14},{9,15},{10,... | collective-permute-start | bytes 1179656 | tf_op jit(solution)/shard_map/ppermute | solution.py:389
  (27 other events, 346.1 us)
